TPU v7x, 512 devices: a whole 4x4x16 slice. The times are simulated.
512 devices in a mesh: row: 64 (over z, y_lo, core), grp: 8 (over y_hi, x).
Axes of the slice: x: 4, y: 4 (y_hi: 2, y_lo: 2; y = y_hi * 2 + y_lo), z: 16, core: 2. Of those that a mesh axis runs over, the one named last changes fastest.
Arguments:
- tokens: bfloat16 [128, 256, 1024], P('row', None, 'grp')
- spec_first: float32 [2, 1024, 128], P(None, 'grp'), may hold values from -0.5 to 0.5
- spec_second: float32 [2, 1024, 128], P(None, 'grp')
- up_weight: bfloat16 [1024, 4096], P(None, 'grp'), may hold values from -0.1875 to 0.1875
- down_weight: bfloat16 [4096, 1024], P('grp'), may hold values from -0.09375 to 0.09375
- head_weight: bfloat16 [1024, 128], P('grp'), may hold values from -0.1875 to 0.1875
- ocean_vel: float32 [2, 1024, 2048], P(None, 'row', 'grp'), may hold values from -4 to 4
- land_mask: int32 [1024, 2048], P('row', 'grp'), may hold values 0 or 1
- ice_mask: int32 [1024, 2048], P('row', 'grp'), may hold values 0 or 1
Outputs:
- block_out: bfloat16 [128, 256, 1024], P('row', None, 'grp')
- ocean_next: float32 [2, 1024, 2048], P(None, 'row', 'grp')
All inputs are finite; a program needn't handle non-finite values. No bound on the sum of `land_mask` or of `ice_mask` on one device may be relied on, other than what follows from the above.
Results may differ from a plain program's by a relative error of at most 0.0085.
Values may be sent and summed in bfloat16 or wider, within the bound.
A program may use at most 64 MiB of HBM per device.

v0:
```python
import math

import jax
import jax.numpy as jnp
from jax import lax
from jax.sharding import PartitionSpec as P

PATCH = 8


highest = lax.Precision.HIGHEST
epsilon = 1e-05
shrink_level = 0.01
drag_coef = 0.25
time_step = 0.5
coriolis = 0.3
viscosity = 1.0
speed_floor = 0.01


def padded_2(array, sides, width):
    for axis, dim in sides:
        peers, length = (lax.axis_size(axis), array.shape[dim])
        up = [(i, (i + 1) % peers) for i in range(peers - 1)]
        down = [(j, i) for i, j in up]
        last = lax.slice_in_dim(array, length - width, length, axis=dim)
        initial = lax.slice_in_dim(array, 0, width, axis=dim)
        before = lax.ppermute(last, axis, up)
        after = lax.ppermute(initial, axis, down)
        array = jnp.concatenate([before, array, after], axis=dim)
    return array


def dft_table(row_count, length, period):
    products = (
        jnp.arange(row_count, dtype=jnp.int32)[:, None]
        * jnp.arange(length, dtype=jnp.int32)[None, :]
        % period
    )
    angles = products.astype(jnp.float32) * (2.0 * math.pi / period)
    return (jnp.cos(angles), jnp.sin(angles))


def normalize(values, totals, channels):
    first = totals[0] / channels
    second = totals[1] / channels
    return (values - first[..., None]) * lax.rsqrt(second - first * first + epsilon)[..., None]


def soft_shrink(values):
    return values - jnp.clip(values, -shrink_level, shrink_level)


def block_mix(real_part, imag_part, spec_first, spec_second, block_size):
    base_shape = real_part.shape
    local_blocks = base_shape[-1] // block_size
    real_part = real_part.reshape(base_shape[:-1] + (local_blocks, block_size))
    imag_part = imag_part.reshape(base_shape[:-1] + (local_blocks, block_size))
    first = spec_first.reshape(2, local_blocks, block_size, block_size)
    second = spec_second.reshape(2, local_blocks, block_size, block_size)

    def apply_block(values, matrix):
        return jnp.einsum("qkbi,bij->qkbj", values, matrix, precision=highest)

    hid_real = jax.nn.relu(apply_block(real_part, first[0]) - apply_block(imag_part, first[1]))
    hid_imag = jax.nn.relu(apply_block(real_part, first[1]) + apply_block(imag_part, first[0]))
    out_real = soft_shrink(apply_block(hid_real, second[0]) - apply_block(hid_imag, second[1]))
    out_imag = soft_shrink(apply_block(hid_real, second[1]) + apply_block(hid_imag, second[0]))
    return (out_real.reshape(base_shape), out_imag.reshape(base_shape))


def apply_rows(table, values):
    return jnp.einsum("qh,hkc->qkc", table, values, precision=highest)


def body(
    tokens,
    spec_first,
    spec_second,
    up_weight,
    down_weight,
    head_weight,
    ocean_vel,
    land_mask,
    ice_mask,
):
    rows_dev, width, channels = tokens.shape
    groups = lax.axis_size("grp")
    total_channels = channels * groups
    height = rows_dev * lax.axis_size("row")
    mode_count = width // 2
    block_size = spec_first.shape[2]
    token_count = rows_dev * width
    inputs = tokens.astype(jnp.float32)
    first_sums = lax.psum((jnp.sum(inputs, axis=2), jnp.sum(inputs * inputs, axis=2)), "grp")
    normed = normalize(inputs, first_sums, total_channels)
    cos_w, sin_w = dft_table(mode_count, width, width)
    norm_scale = 1.0 / math.sqrt(height * width)
    spectra_real = jnp.einsum("kw,hwc->hkc", cos_w, normed, precision=highest) * norm_scale
    spectra_imag = -jnp.einsum("kw,hwc->hkc", sin_w, normed, precision=highest) * norm_scale
    col_real, col_imag = (
        lax.all_to_all(spectra_real, "row", split_axis=1, concat_axis=0, tiled=True),
        lax.all_to_all(spectra_imag, "row", split_axis=1, concat_axis=0, tiled=True),
    )
    cos_h, sin_h = dft_table(height, height, height)
    freq_real = apply_rows(cos_h, col_real) + apply_rows(sin_h, col_imag)
    freq_imag = apply_rows(cos_h, col_imag) - apply_rows(sin_h, col_real)
    mix_real, mix_imag = block_mix(freq_real, freq_imag, spec_first, spec_second, block_size)
    back_real = apply_rows(cos_h, mix_real) - apply_rows(sin_h, mix_imag)
    back_imag = apply_rows(cos_h, mix_imag) + apply_rows(sin_h, mix_real)
    row_real, row_imag = (
        lax.all_to_all(back_real, "row", split_axis=0, concat_axis=1, tiled=True),
        lax.all_to_all(back_imag, "row", split_axis=0, concat_axis=1, tiled=True),
    )
    doubling = jnp.where(jnp.arange(mode_count) == 0, 1.0, 2.0).astype(jnp.float32)[:, None]
    filtered = (
        jnp.einsum("kw,hkc->hwc", cos_w * doubling, row_real, precision=highest)
        - jnp.einsum("kw,hkc->hwc", sin_w * doubling, row_imag, precision=highest)
    ) * norm_scale
    mixed_in = inputs + normed + filtered
    second_sums = lax.psum((jnp.sum(mixed_in, axis=2), jnp.sum(mixed_in * mixed_in, axis=2)), "grp")
    normed_two = normalize(mixed_in, second_sums, total_channels).astype(jnp.bfloat16)
    flat_norm = normed_two.reshape(token_count, channels)
    hidden_pre = jnp.dot(
        lax.all_gather(flat_norm, "grp", axis=1, tiled=True),
        up_weight,
        preferred_element_type=jnp.float32,
    )
    hidden = jax.nn.gelu(hidden_pre, approximate=False).astype(jnp.bfloat16)
    tile_width = width // groups
    partial_value = jnp.dot(hidden, down_weight, preferred_element_type=jnp.float32)
    summed = lax.psum_scatter(
        partial_value.astype(jnp.bfloat16), "grp", scatter_dimension=1, tiled=True
    ).astype(jnp.float32)
    flat_out = (mixed_in.reshape(token_count, channels) + summed).astype(jnp.bfloat16)
    head_part = jnp.dot(flat_out, head_weight, preferred_element_type=jnp.float32)
    own_comps = lax.psum_scatter(head_part, "grp", scatter_dimension=1, tiled=True)
    all_comps = lax.all_gather(own_comps, "grp", axis=1, tiled=True)
    velocity = lax.dynamic_slice_in_dim(
        all_comps.reshape(rows_dev, width, head_part.shape[1]),
        lax.axis_index("grp") * tile_width,
        tile_width,
        1,
    )
    block_out = flat_out.reshape(rows_dev, width, channels)
    ice_vel = (
        velocity.reshape(rows_dev, tile_width, 2, PATCH, PATCH)
        .transpose(2, 0, 3, 1, 4)
        .reshape(2, rows_dev * PATCH, tile_width * PATCH)
    )
    land_open = land_mask.astype(jnp.float32)
    ice_cover = ice_mask.astype(jnp.float32)
    ocean_now = ocean_vel * land_open[None]
    padded = padded_2(ocean_now, (("row", 1), ("grp", 2)), 1)
    center = padded[:, 1:-1, 1:-1]
    laplace = (
        padded[:, 2:, 1:-1]
        + padded[:, :-2, 1:-1]
        + padded[:, 1:-1, 2:]
        + padded[:, 1:-1, :-2]
        - 4.0 * center
    )
    relative = ice_vel - ocean_now
    drift_speed = jnp.sqrt(relative[0] * relative[0] + relative[1] * relative[1] + speed_floor)
    stress = drag_coef * (ice_cover * drift_speed)[None] * relative
    rotated = jnp.stack([ocean_now[1], -ocean_now[0]])
    ocean_next = land_open[None] * (
        ocean_now + time_step * (coriolis * rotated + stress + viscosity * laplace)
    )
    return (block_out, ocean_next)


def solution(mesh):
    placed = (
        P("row", None, "grp"),
        P(None, "grp", None),
        P(None, "grp", None),
        P(None, "grp"),
        P("grp", None),
        P("grp", None),
        P(None, "row", "grp"),
        P("row", "grp"),
        P("row", "grp"),
    )
    return jax.shard_map(
        body,
        mesh=mesh,
        in_specs=placed,
        out_specs=(P("row", None, "grp"), P(None, "row", "grp")),
        check_vma=False,
    )
```

profile of v0, /device:TPU:6, one launch (start us, length us, event | category | flops | bytes accessed | tf_op | source)
XLA Modules:
  0.0 453.8 jit_solution(15744712399999976966)
XLA Ops:
  7.2 1.1 copy.29
  8.3 0.1 convert_reduce_fusion
  8.3 20.6 %all-reduce.1 = (f32[2,256]{1,0:T(2,128)S(1)}, f32[2,256]{1,0:T(2,128)S(1)}) all-reduce(f32[2,256]{1,0:T(2,128)S(1)} %get-tuple-element.5, f32[2,256]{1,0:T(2,128)S(1)} %get-tuple-element.4), channel_id=1, replica_groups=mesh['row'=64,'grp'=8] {'grp'}, use_global_device_ids=true, to_apply=%region_3.0 | all-reduce | flops 1024 | bytes 8192 | tf_op jit(solution)/shard_map/psum | solution.py:95
  28.9 0.9 fusion.4
  29.8 0.8 copy.33
  30.6 15.2 %all-to-all-start.1 = ((f32[2,128,128]{2,0,1:T(2,128)}), f32[2,128,128]{2,0,1:T(2,128)S(1)}, u32[]{:S(2)}, u32[]{:S(2)}) async-start(f32[2,128,128]{2,0,1:T(2,128)} %copy.33), calls=%async_computation.1 | async-start | bytes 262144 | tf_op jit(solution)/shard_map/all_to_all | solution.py:103
  45.8 0.9 fusion.5
  46.7 0.8 copy.30
  47.4 15.4 %all-to-all-done.1 = f32[2,128,128]{2,0,1:T(2,128)S(1)} async-done(((f32[2,128,128]{2,0,1:T(2,128)}), f32[2,128,128]{2,0,1:T(2,128)S(1)}, u32[]{:S(2)}, u32[]{:S(2)}) %all-to-all-start.1) | async-done | bytes 131104 | tf_op jit(solution)/shard_map/all_to_all | solution.py:103
  62.8 4.6 %all-to-all-start = ((f32[2,128,128]{2,0,1:T(2,128)}), f32[2,128,128]{2,0,1:T(2,128)S(1)}, u32[]{:S(2)}, u32[]{:S(2)}) async-start(f32[2,128,128]{2,0,1:T(2,128)} %copy.30), calls=%async_computation | async-start | bytes 262144 | tf_op jit(solution)/shard_map/all_to_all | solution.py:102
  67.5 0.1 copy.35
  67.6 0.5 fusion.98
  68.1 16.4 %all-to-all-done = f32[2,128,128]{2,0,1:T(2,128)S(1)} async-done(((f32[2,128,128]{2,0,1:T(2,128)}), f32[2,128,128]{2,0,1:T(2,128)S(1)}, u32[]{:S(2)}, u32[]{:S(2)}) %all-to-all-start) | async-done | bytes 131104 | tf_op jit(solution)/shard_map/all_to_all | solution.py:102
  84.5 0.1 copy.32
  84.6 0.5 fusion.100
  85.1 0.5 convolution_add_fusion.3
  85.7 0.3 fusion.84
  85.9 0.3 fusion.88
  86.2 0.5 convolution_subtract_fusion.4
  86.7 0.3 fusion.8
  87.0 0.3 fusion.78
  87.3 0.3 fusion.82
  87.5 0.3 fusion.9
  87.8 0.3 fusion.56
  88.1 0.5 fusion.94
  88.6 0.3 fusion.57
  88.9 0.5 convolution_add_fusion
  89.4 0.8 copy.39
  90.1 4.6 %all-to-all-start.3 = ((f32[128,2,128]{2,1,0:T(2,128)}), f32[128,2,128]{2,1,0:T(2,128)S(1)}, u32[]{:S(2)}, u32[]{:S(2)}) async-start(f32[128,2,128]{2,1,0:T(2,128)} %copy.39), calls=%async_computation.3 | async-start | bytes 262144 | tf_op jit(solution)/shard_map/all_to_all | solution.py:113
  94.8 0.5 fusion.96
  95.3 0.5 convolution_subtract_fusion.1
  95.8 0.8 copy.36
  96.5 15.2 %all-to-all-done.3 = f32[128,2,128]{2,1,0:T(2,128)S(1)} async-done(((f32[128,2,128]{2,1,0:T(2,128)}), f32[128,2,128]{2,1,0:T(2,128)S(1)}, u32[]{:S(2)}, u32[]{:S(2)}) %all-to-all-start.3) | async-done | bytes 131104 | tf_op jit(solution)/shard_map/all_to_all | solution.py:113
  111.8 4.6 %all-to-all-start.2 = ((f32[128,2,128]{2,1,0:T(2,128)}), f32[128,2,128]{2,1,0:T(2,128)S(1)}, u32[]{:S(2)}, u32[]{:S(2)}) async-start(f32[128,2,128]{2,1,0:T(2,128)} %copy.36), calls=%async_computation.2 | async-start | bytes 262144 | tf_op jit(solution)/shard_map/all_to_all | solution.py:112
  116.4 0.2 all-gather.2.cloned.1.call-start
  116.7 16.7 %all-to-all-done.2 = f32[128,2,128]{2,1,0:T(2,128)S(1)} async-done(((f32[128,2,128]{2,1,0:T(2,128)}), f32[128,2,128]{2,1,0:T(2,128)S(1)}, u32[]{:S(2)}, u32[]{:S(2)}) %all-to-all-start.2) | async-done | bytes 131104 | tf_op jit(solution)/shard_map/all_to_all | solution.py:112
  133.5 0.9 fusion.62
  134.4 0.9 fusion.224
  135.3 21.8 %all-reduce = (f32[2,256]{1,0:T(2,128)S(1)}, f32[2,256]{1,0:T(2,128)S(1)}) all-reduce(f32[2,256]{1,0:T(2,128)S(1)} %get-tuple-element.3, f32[2,256]{1,0:T(2,128)S(1)} %get-tuple-element.2), channel_id=1, replica_groups=mesh['row'=64,'grp'=8] {'grp'}, use_global_device_ids=true, to_apply=%region_7.8 | all-reduce | flops 1024 | bytes 8192 | tf_op jit(solution)/shard_map/psum | solution.py:121
  157.2 0.8 copy.43
  157.9 0.0 all-gather.2.cloned.1.call-update
  158.0 0.0 reduce-scatter.7.cloned.1.call-start
  158.0 54.7 %all-gather.2.cloned.1.call-done = bf16[512,1024]{1,0:T(8,128)(2,1)} async-done(((bf16[512,128]{1,0:T(8,128)(2,1)}), bf16[512,1024]{1,0:T(8,128)(2,1)}) %all-gather.2.cloned.1.call-update) | async-done | bytes 1048592 | tf_op jit(solution)/shard_map/all_gather | solution.py:125
  212.7 4.6 %convolution_convert_fusion = bf16[512,1024]{1,0:T(8,128)(2,1)S(1)} fusion(bf16[512,1024]{1,0:T(8,128)(2,1)S(1)} %copy-done, bf16[512,1024]{1,0:T(8,128)(2,1)} %all-gather.2.cloned.1.call-done, bf16[1024,512]{1,0:T(8,128)(2,1)S(1)} %copy-done.8), kind=kOutput, calls=%fused_computation.1 | convolution fusion | flops 1091305472 | bytes 4194304 | tf_op jit(solution)/shard_map/dot_general | solution.py:131
  217.4 1.3 copy.48
  218.7 0.0 reduce-scatter.5.cloned.1.call-start
  218.8 0.1 copy.42
  218.9 86.2 %reduce-scatter.7.cloned.1.call-done = bf16[128,512]{1,0:T(8,128)(2,1)} async-done(((bf16[1024,512]{1,0:T(8,128)(2,1)}), bf16[128,512]{1,0:T(8,128)(2,1)}) %reduce-scatter.7.cloned.1.call-update) | async-done | bytes 131088
  305.1 1.0 copy.49
  306.2 0.9 fusion.231
  307.2 87.6 %reduce-scatter.5.cloned.1.call-done = f32[512,16]{0,1:T(8,128)} async-done(((f32[512,128]{0,1:T(8,128)}), f32[512,16]{0,1:T(8,128)}) %reduce-scatter.5.cloned.1.call-update) | async-done | bytes 32784 | tf_op jit(solution)/shard_map/reduce_scatter | solution.py:137
  394.8 34.6 %all_gather.7 = f32[512,128]{0,1:T(8,128)S(1)} all-gather(f32[512,16]{0,1:T(8,128)} %reduce-scatter.5.cloned.1.call-done), channel_id=1, replica_groups=mesh['row'=64,'grp'=8] {'grp'}, dimensions={1}, use_global_device_ids=true | all-gather | bytes 294912 | tf_op jit(solution)/shard_map/all_gather | solution.py:138
  429.4 0.2 reshape.111
  429.6 0.2 constant_dynamic-slice_fusion
  429.8 0.2 copy.45
  430.0 0.3 reshape.113
  430.3 1.3 collective-permute-start
  431.6 3.0 collective-permute-start.1
  434.7 0.8 collective-permute-done.1
  435.5 0.1 fusion.226
  435.6 1.9 collective-permute-start.2
  437.5 7.5 %collective-permute-start.3 = (f32[2,18,1]{2,1,0:T(8,128)S(1)}, f32[2,18,1]{2,1,0:T(8,128)S(1)}, u32[]{:S(2)}, u32[]{:S(2)}) collective-permute-start(f32[2,18,1]{2,1,0:T(8,128)S(1)} %get-tuple-element.13), channel_id=1, source_target_pairs={{0,1},{1,2},{2,3},{3,4},{4,5},{5,6},{6,7},{8,9},{9,10},{10,11},{11... | collective-permute-start | bytes 440 | tf_op jit(solution)/shard_map/ppermute | solution.py:28
  445.1 1.5 collective-permute-done.3
  446.5 0.7 fusion.126
  (38 shorter events, 0.4 us)
Async XLA Ops:
  7.2 205.6 %copy-start = (bf16[512,1024]{1,0:T(8,128)(2,1)S(1)}, bf16[512,1024]{1,0:T(8,128)(2,1)}, u32[]{:S(2)}) copy-start(bf16[512,1024]{1,0:T(8,128)(2,1)} %param.13) | copy-start | bytes 3145732
  30.6 32.3 %all-to-all-start.1 = ((f32[2,128,128]{2,0,1:T(2,128)}), f32[2,128,128]{2,0,1:T(2,128)S(1)}, u32[]{:S(2)}, u32[]{:S(2)}) async-start(f32[2,128,128]{2,0,1:T(2,128)} %copy.33), calls=%async_computation.1 | async-start | bytes 262144 | tf_op jit(solution)/shard_map/all_to_all | solution.py:103
  62.8 21.6 %all-to-all-start = ((f32[2,128,128]{2,0,1:T(2,128)}), f32[2,128,128]{2,0,1:T(2,128)S(1)}, u32[]{:S(2)}, u32[]{:S(2)}) async-start(f32[2,128,128]{2,0,1:T(2,128)} %copy.30), calls=%async_computation | async-start | bytes 262144 | tf_op jit(solution)/shard_map/all_to_all | solution.py:102
  67.5 18.2 %copy-start.1 = (f32[2,128,128]{2,1,0:T(8,128)S(1)}, f32[2,128,128]{2,1,0:T(8,128)}, u32[]{:S(2)}) copy-start(f32[2,128,128]{2,1,0:T(8,128)} %param.10) | copy-start | bytes 393220
  84.6 2.4 copy-start.2
  90.1 21.6 %all-to-all-start.3 = ((f32[128,2,128]{2,1,0:T(2,128)}), f32[128,2,128]{2,1,0:T(2,128)S(1)}, u32[]{:S(2)}, u32[]{:S(2)}) async-start(f32[128,2,128]{2,1,0:T(2,128)} %copy.39), calls=%async_computation.3 | async-start | bytes 262144 | tf_op jit(solution)/shard_map/all_to_all | solution.py:113
  111.8 21.6 %all-to-all-start.2 = ((f32[128,2,128]{2,1,0:T(2,128)}), f32[128,2,128]{2,1,0:T(2,128)S(1)}, u32[]{:S(2)}, u32[]{:S(2)}) async-start(f32[128,2,128]{2,1,0:T(2,128)} %copy.36), calls=%async_computation.2 | async-start | bytes 262144 | tf_op jit(solution)/shard_map/all_to_all | solution.py:112
  116.4 96.3 %all-gather.2.cloned.1.call-start = ((), (), s32[]{:S(2)}) async-start(), calls=%async_computation.6 | async-start | bytes 1179648 | tf_op jit(solution)/shard_map/all_gather | solution.py:125
  134.3 78.4 %copy-start.8 = (bf16[1024,512]{1,0:T(8,128)(2,1)S(1)}, bf16[1024,512]{1,0:T(8,128)(2,1)}, u32[]{:S(2)}) copy-start(bf16[1024,512]{1,0:T(8,128)(2,1)} %param.12) | copy-start | bytes 3145732
  158.0 147.1 %reduce-scatter.7.cloned.1.call-start = ((), (), s32[]{:S(2)}) async-start(), calls=%async_computation.8 | async-start | bytes 1179648
  218.7 87.5 %copy-start.5 = (bf16[128,128]{1,0:T(8,128)(2,1)S(1)}, bf16[128,128]{1,0:T(8,128)(2,1)}, u32[]{:S(2)}) copy-start(bf16[128,128]{1,0:T(8,128)(2,1)} %param.14) | copy-start | bytes 98308
  218.7 88.4 %copy-start.6 = (s32[16,256]{1,0:T(8,128)S(1)}, s32[16,256]{1,0:T(8,128)}, u32[]{:S(2)}) copy-start(s32[16,256]{1,0:T(8,128)} %param.16) | copy-start | bytes 49156
  218.7 176.0 %reduce-scatter.5.cloned.1.call-start = ((), (), s32[]{:S(2)}) async-start(), calls=%async_computation.7 | async-start | bytes 294912 | tf_op jit(solution)/shard_map/reduce_scatter | solution.py:137
  306.2 123.8 %copy-start.3 = (bf16[512,128]{1,0:T(8,128)(2,1)}, bf16[512,128]{1,0:T(8,128)(2,1)S(1)}, u32[]{:S(2)}) copy-start(bf16[512,128]{1,0:T(8,128)(2,1)S(1)} %fusion.55) | copy-start | bytes 393220
  429.4 0.9 copy-start.4
  429.6 15.5 %copy-start.7 = (s32[16,256]{1,0:T(8,128)S(1)}, s32[16,256]{1,0:T(8,128)}, u32[]{:S(2)}) copy-start(s32[16,256]{1,0:T(8,128)} %param.17) | copy-start | bytes 49156
  430.3 4.4 collective-permute-start
  431.6 3.8 collective-permute-start.1
  435.6 9.5 %collective-permute-start.2 = (f32[2,18,1]{2,1,0:T(8,128)S(1)}, f32[2,18,1]{2,1,0:T(8,128)S(1)}, u32[]{:S(2)}, u32[]{:S(2)}) collective-permute-start(f32[2,18,1]{2,1,0:T(8,128)S(1)} %get-tuple-element.12), channel_id=1, source_target_pairs={{1,0},{2,1},{3,2},{4,3},{5,4},{6,5},{7,6},{9,8},{10,9},{11,10},{12... | collective-permute-start | bytes 440 | tf_op jit(solution)/shard_map/ppermute | solution.py:29
  437.5 9.0 %collective-permute-start.3 = (f32[2,18,1]{2,1,0:T(8,128)S(1)}, f32[2,18,1]{2,1,0:T(8,128)S(1)}, u32[]{:S(2)}, u32[]{:S(2)}) collective-permute-start(f32[2,18,1]{2,1,0:T(8,128)S(1)} %get-tuple-element.13), channel_id=1, source_target_pairs={{0,1},{1,2},{2,3},{3,4},{4,5},{5,6},{6,7},{8,9},{9,10},{10,11},{11... | collective-permute-start | bytes 440 | tf_op jit(solution)/shard_map/ppermute | solution.py:28
Sparse Core Ops, SparseCore 0:
  158.1 54.6 all-gather.1
  218.8 86.2 reduce-scatter.6
  310.2 84.5 reduce-scatter.4
where the time goes:
time: 460 us; the launch traced here: 454 us
  waiting for transfers between devices  295 us (64%)
  blocking collectives  77 us (17%)
  starting transfers between devices  43.2 us (9%)
  matrix products  15.3 us (3%)
  between operations  14.2 us (3%)
  local copies, waits for them, and re-layouts  8.69 us (2%)
    reduce_scatter x1, waiting for transfers between devices, body(): lax.psum_scatter(head_part, 'grp', scatter_dimension=1, tiled=True)  87.6 us
    unnamed x4, waiting for transfers between devices  86.2 us
    all_gather x1, waiting for transfers between devices, body(): lax.all_gather(flat_norm, 'grp', axis=1, tiled=True)  54.7 us
    all_gather x1, blocking collectives, body(): all_comps = lax.all_gather(own_comps, 'grp', axis=1, tiled=True)  34.6 us
    psum x1, blocking collectives, body(): lax.psum((jnp.sum(mixed_in, axis=2), jnp.sum(mixed_in * mixed_in, axis=2)...  21.8 us
    psum x1, blocking collectives, body(): lax.psum((jnp.sum(inputs, axis=2), jnp.sum(inputs * inputs, axis=2)), 'grp')  20.6 us
    all_to_all x1, waiting for transfers between devices, body(): lax.all_to_all(back_real, 'row', split_axis=0, concat_axis=1, tiled=True)  16.7 us
    all_to_all x1, waiting for transfers between devices, body(): lax.all_to_all(spectra_real, 'row', split_axis=1, concat_axis=0, tiled=True)  16.4 us
  transfers between devices with their start and end apart: 11, of which 9 were waited for; matrix products, arithmetic and copies ran while one was open for 1% of the time, Pallas kernels for 0%

commit v1 on v0

v1 whole, which is shorter than its diff:
```python
import functools
import math

import jax
import jax.numpy as jnp
import ml_dtypes
import numpy as np
from jax import lax
from jax.experimental import pallas as pl
from jax.experimental.pallas import tpu as pltpu
from jax.sharding import PartitionSpec as P

PATCH = 8
C = 128

epsilon = 1e-05
shrink_level = 0.01
drag_coef = 0.25
time_step = 0.5
coriolis = 0.3
viscosity = 1.0
speed_floor = 0.01

F32 = jnp.float32
BF16 = jnp.bfloat16
MESH = pl.DeviceIdType.MESH


def dft_tables(planes):
    height, width = 8 * planes, 16 * planes
    size = 16 * planes
    row = np.arange(size)
    k, part = row // 2, row % 2
    angle = 2.0 * np.pi * ((k[:, None] * np.arange(width)[None, :]) % width) / width
    row_fwd = np.where(part[:, None] == 0, np.cos(angle), -np.sin(angle))
    row_bwd = np.where(k == 0, 1.0, 2.0)[None, :] * row_fwd.T
    regroup = np.zeros((size, size))
    at = 0
    for q in range(4):
        for kk in range(2):
            for z in range(planes):
                for part_at in range(2):
                    regroup[at, z * 16 + (2 * q + kk) * 2 + part_at] = 1.0
                    at += 1
    col = np.array(
        [(8 * z + 2 * q + r, p) for r in range(2) for q in range(4) for z in range(planes) for p in range(2)]
    )
    col_h, col_part = col[:, 0], col[:, 1]
    angle = 2.0 * np.pi * ((np.arange(height)[:, None] * col_h[None, :]) % height) / height
    cos, sin = np.cos(angle), np.sin(angle)
    real = np.where(col_part[None, :] == 0, cos, sin)
    imag = np.where(col_part[None, :] == 0, -sin, cos)
    col_fwd = np.concatenate([real, imag], axis=0)
    tables = [row_fwd, regroup, col_fwd, col_fwd.T, regroup.T, row_bwd]
    return np.concatenate(tables, axis=0).astype(ml_dtypes.bfloat16)


def dot(a, b):
    return jnp.dot(a, b, preferred_element_type=F32)


def dot_nt(a, b):
    return lax.dot_general(a, b, (((1,), (1,)), ((), ())), preferred_element_type=F32)


def split_hi_lo(values):
    hi = values.astype(BF16)
    return hi, (values - hi.astype(F32)).astype(BF16)


def soft_shrink(values):
    return values - jnp.clip(values, -shrink_level, shrink_level)


def gelu(values):
    return 0.5 * values * (1.0 + lax.erf(values * (1.0 / math.sqrt(2.0))))


def far_first(count):
    return sorted(range(1, count), key=lambda i: -min(i, count - i))


def complex_matrix(ref):
    real, imag = ref[0], ref[1]
    top = jnp.concatenate([real, imag], axis=1)
    low = jnp.concatenate([-imag, real], axis=1)
    return jnp.concatenate([top, low], axis=0)


def stack_rows(rows, count, width):
    at = lax.broadcasted_iota(jnp.int32, (count, width), 0)
    out = jnp.zeros((count, width), F32)
    for i, values in enumerate(rows):
        out = jnp.where(at == i, values, out)
    return out


def columns_of(rows, width):
    top = stack_rows(rows, 8, width)
    return jnp.concatenate([top, jnp.zeros((C - 8, width), F32)], axis=0).T


def kernel(
    planes,
    groups,
    tok_hbm, first_hbm, second_hbm, up_hbm, down_hbm, head_hbm, vel_hbm, land_hbm, ice_hbm, tab_hbm,
    bo_hbm, oc_hbm,
    tok, first, second, up, down, head, vel, land, ice, tab,
    st1_send, st1_recv, z1_send, z1_recv, p1_send, p1_recv, p2_send, p2_recv, z2_send, z2_recv,
    mixed, y_send, y_recv, st2_send, st2_recv, peer_up, peer_down, hid_own, hid_peer, rs_send, rs_recv,
    bo, bo_recv, hw_send, hw_recv, now, halo_up, halo_down, halo_left, halo_right, ocean,
    local_sem, send_sem, recv_sem, out_sem,
):
    width = tok.shape[1]
    across = groups // 2
    total_channels = C * groups
    row, grp = lax.axis_index("row"), lax.axis_index("grp")
    rows = 4 * planes
    z, q = row // 4, row % 4
    y_lo, core = q // 2, q % 2
    y_hi, x = grp // across, grp % across
    hidden = up.shape[1]

    loads = {}
    for i, (name, src, dst) in enumerate(
        [
            ("tok", tok_hbm, tok),
            ("tab", tab_hbm, tab),
            ("vel", vel_hbm, vel),
            ("land", land_hbm, land),
            ("head", head_hbm, head),
            ("first", first_hbm, first),
            ("second", second_hbm, second),
            ("up", up_hbm, up),
            ("down", down_hbm, down),
            ("ice", ice_hbm, ice),
        ]
    ):
        loads[name] = pltpu.make_async_copy(src, dst, local_sem.at[i])
        loads[name].start()

    z_peers = [(lax.rem(z + i, planes) * 4 + q, grp) for i in far_first(planes)]
    q_peers = [(z * 4 + (q + i) % 4, grp) for i in (2, 3, 1)]
    g_peers = [lax.rem(grp + i, groups) for i in far_first(groups)]
    row_above, row_below = lax.rem(row + rows - 1, rows), lax.rem(row + 1, rows)
    weight_peer = (z * 4 + (1 - y_lo) * 2 + core, (1 - y_hi) * across + x)
    sibling = (z * 4 + y_lo * 2 + (1 - core), grp)
    greeted = z_peers + q_peers + [(row, g) for g in g_peers]
    greeted += [(row_above, grp), (row_below, grp), weight_peer]
    barrier = pltpu.get_barrier_semaphore()
    for peer in greeted:
        pl.semaphore_signal(barrier, inc=1, device_id=peer, device_id_type=MESH)

    ones = jnp.ones((16, C), BF16)
    loads["tok"].wait()
    sums = []
    squares = []
    for r in range(2):
        values = tok[r]
        wide = values.astype(F32)
        hi, lo = split_hi_lo(wide * wide)
        sums.append(dot_nt(ones, values)[0:1])
        squares.append((dot_nt(ones, hi) + dot_nt(ones, lo))[0:1])
    st1_send[...] = stack_rows(sums + squares, 8, width)
    st1_recv[grp] = st1_send[...]
    loads["head"].wait()
    hw_send[...] = head[...].astype(F32).T.astype(BF16)
    hw_recv[grp] = hw_send[...]
    loads["vel"].wait()
    loads["land"].wait()
    open_water = land[...].astype(F32)
    now[0] = vel[0] * open_water
    now[1] = vel[1] * open_water

    pl.semaphore_wait(barrier, len(greeted))

    drains = []

    def send(src, dst, at, peer):
        pltpu.make_async_remote_copy(
            src_ref=src,
            dst_ref=dst,
            send_sem=send_sem.at[at],
            recv_sem=recv_sem.at[at],
            device_id=peer,
            device_id_type=MESH,
        ).start()

    def wait_on(sem, like):
        pltpu.make_async_copy(like, like, sem).wait()

    def arrived(at, like):
        wait_on(recv_sem.at[at], like)
        drains.append((at, like))

    ST1, WUP, WDN, HW, HUP, HDN, HLF, HRT, Z1, P1, P2, Z2, Y, ST2, FUP, FDN, RS, BO = range(18)

    for g in g_peers:
        send(st1_send, st1_recv.at[grp], ST1, (row, g))
    half_up = pl.ds(pl.multiple_of(core * (up.shape[0] // 2), up.shape[0] // 2), up.shape[0] // 2)
    half_dn = pl.ds(pl.multiple_of(core * (hidden // 2), hidden // 2), hidden // 2)
    send(up_hbm.at[half_up], peer_up.at[half_up], WUP, weight_peer)
    send(down_hbm.at[half_dn], peer_down.at[half_dn], WDN, weight_peer)

    arrived(ST1, st1_recv.at[pl.ds(0, groups - 1)])
    totals = st1_recv[0]
    for g in range(1, groups):
        totals = totals + st1_recv[g]
    totals = totals / total_channels
    mean, mean_square = totals[0:2], totals[2:4]
    scale = lax.rsqrt(mean_square - mean * mean + epsilon)
    stats = columns_of([mean[0:1], mean[1:2], scale[0:1], scale[1:2]], width)
    loads["tab"].wait()
    size = 16 * planes

    def table(i):
        return tab[i * size : (i + 1) * size]

    normed = []
    for r in range(2):
        inputs = tok[r].astype(F32)
        normed.append((inputs - stats[:, r : r + 1]) * stats[:, 2 + r : 3 + r])
        mixed[r] = inputs + normed[r]

    flat = jnp.concatenate([normed[0].astype(BF16), normed[1].astype(BF16)], axis=1)
    row_scale, col_scale = 1.0 / math.sqrt(width), 1.0 / math.sqrt(8 * planes)
    z1_send[...] = (dot(table(0), flat) * row_scale).astype(BF16).reshape(planes, 16, 2 * C)
    for peer in z_peers:
        send(z1_send.at[peer[0] // 4], z1_recv.at[z], Z1, peer)
    z1_recv[z] = z1_send[z]

    for g in g_peers:
        send(hw_send, hw_recv.at[grp], HW, (row, g))
    send(now.at[:, pl.ds(8, 8)], halo_up, HUP, (row_below, grp))
    send(now.at[:, pl.ds(0, 8)], halo_down, HDN, (row_above, grp))
    lanes = now.shape[2]
    send(now.at[:, :, pl.ds(lanes - C, C)], halo_left, HLF, (row, lax.rem(grp + 1, groups)))
    send(now.at[:, :, pl.ds(0, C)], halo_right, HRT, (row, lax.rem(grp + groups - 1, groups)))
    loads["first"].wait()
    loads["second"].wait()
    weight_one = complex_matrix(first).astype(BF16)
    weight_two, weight_two_lo = split_hi_lo(complex_matrix(second))
    loads["up"].wait()
    loads["down"].wait()
    loads["ice"].wait()
    block_at = lax.broadcasted_iota(jnp.int32, (16, total_channels), 0)
    block_of = lax.broadcasted_iota(jnp.int32, (16, total_channels), 1) // C
    pick = jnp.where(block_at == block_of, 1.0, 0.0).astype(BF16)

    def column_sums(weights):
        sums = dot(pick, weights)
        hi, lo = split_hi_lo(sums)
        pad = jnp.zeros((C - 16, hidden), BF16)
        return jnp.concatenate([hi, pad], axis=0), jnp.concatenate([lo, pad], axis=0)

    own_sums = column_sums(up[...])

    arrived(Z1, z1_recv.at[pl.ds(0, planes - 1)])
    quarter = 4 * planes
    p1_send[...] = dot(table(1), z1_recv[...].reshape(size, 2 * C)).astype(BF16).reshape(4, quarter, 2 * C)
    for peer in q_peers:
        send(p1_send.at[peer[0] % 4], p1_recv.at[q], P1, peer)
    p1_recv[q] = p1_send[q]
    arrived(P1, p1_recv.at[pl.ds(0, 3)])

    half = 2 * planes

    def gathered(kk, r):
        return [p1_recv[q_at, kk * half : (kk + 1) * half, r * C : (r + 1) * C] for q_at in range(4)]

    by_kk = [jnp.concatenate(gathered(kk, 0) + gathered(kk, 1), axis=0) for kk in range(2)]
    freq = (dot(table(2), jnp.concatenate(by_kk, axis=1)) * col_scale).astype(BF16)
    height = 8 * planes

    def swapped(values):
        top = jnp.concatenate([values[:height, :C], values[height:, :C]], axis=1)
        low = jnp.concatenate([values[:height, C:], values[height:, C:]], axis=1)
        return jnp.concatenate([top, low], axis=0)

    hid = jax.nn.relu(dot(swapped(freq), weight_one)).astype(BF16)
    mix = soft_shrink(dot(hid, weight_two) + dot(hid, weight_two_lo)).astype(BF16)
    back = (dot(table(3), swapped(mix)) * col_scale).astype(BF16)
    for q_at in range(4):
        for r in range(2):
            for kk in range(2):
                start = r * height + q_at * half
                p2_send[q_at, kk * half : (kk + 1) * half, r * C : (r + 1) * C] = back[
                    start : start + half, kk * C : (kk + 1) * C
                ]
    for peer in q_peers:
        send(p2_send.at[peer[0] % 4], p2_recv.at[q], P2, peer)
    p2_recv[q] = p2_send[q]
    arrived(P2, p2_recv.at[pl.ds(0, 3)])
    z2_send[...] = dot(table(4), p2_recv[...].reshape(size, 2 * C)).astype(BF16).reshape(planes, 16, 2 * C)
    for peer in z_peers:
        send(z2_send.at[peer[0] // 4], z2_recv.at[z], Z2, peer)
    z2_recv[z] = z2_send[z]
    arrived(Z2, z2_recv.at[pl.ds(0, planes - 1)])
    filtered = dot(table(5), z2_recv[...].reshape(size, 2 * C)) * row_scale

    square_ones = jnp.ones((C, C), BF16)
    for r in range(2):
        values = mixed[r] + filtered[:, r * C : (r + 1) * C]
        mixed[r] = values
        hi = values.astype(BF16)
        local_mean = dot(hi, square_ones) * (1.0 / C)
        centered = (values - local_mean).astype(BF16)
        y_send[r] = centered
        wide = centered.astype(F32)
        sq_hi, sq_lo = split_hi_lo(wide * wide)
        row_mean = dot_nt(ones, hi)[0:1] * (1.0 / C)
        row_sum = dot_nt(ones, centered)[0:1]
        row_square = (dot_nt(ones, sq_hi) + dot_nt(ones, sq_lo))[0:1]
        st2_send[r] = stack_rows([row_mean, row_sum, row_square], 8, width)
    for g in g_peers:
        send(y_send.at[g // across], y_recv.at[grp], Y, (row, g))
        send(st2_send.at[g // across], st2_recv.at[grp], ST2, (row, g))
    y_recv[grp] = y_send[y_hi]
    st2_recv[grp] = st2_send[y_hi]

    wait_on(recv_sem.at[WUP], peer_up.at[pl.ds(0, up.shape[0] // 2)])
    drains.append((WUP, peer_up.at[pl.ds(0, up.shape[0] // 2)]))
    send(peer_up.at[half_up], peer_up.at[half_up], FUP, sibling)
    wait_on(recv_sem.at[WDN], peer_down.at[pl.ds(0, hidden // 2)])
    drains.append((WDN, peer_down.at[pl.ds(0, hidden // 2)]))
    send(peer_down.at[half_dn], peer_down.at[half_dn], FDN, sibling)

    arrived(ST2, st2_recv.at[pl.ds(0, groups - 1)])
    sent = [st2_recv[g] for g in range(groups)]
    mean = sent[0][0:1] + sent[0][1:2] * (1.0 / C)
    for g in range(1, groups):
        mean = mean + (sent[g][0:1] + sent[g][1:2] * (1.0 / C))
    mean = mean * (1.0 / groups)
    offsets = [sent[g][0:1] - mean for g in range(groups)]
    square = jnp.zeros((1, width), F32)
    for g in range(groups):
        square = square + (sent[g][2:3] + 2.0 * offsets[g] * sent[g][1:2] + float(C) * offsets[g] * offsets[g])
    scale = lax.rsqrt(square / total_channels + epsilon)
    off_hi, off_lo = split_hi_lo(columns_of(offsets, width))
    scale = columns_of([scale], width)[:, 0:1]

    arrived(Y, y_recv.at[pl.ds(0, groups - 1)])
    flat = jnp.concatenate([y_recv[g] for g in range(groups)], axis=1)

    def hidden_of(weights, sums):
        shift = dot(off_hi, sums[0]) + dot(off_lo, sums[0]) + dot(off_hi, sums[1])
        return gelu((dot(flat, weights) + shift) * scale).astype(BF16)

    hid_own[...] = hidden_of(up[...], own_sums)
    arrived(FUP, peer_up.at[pl.ds(0, up.shape[0] // 2)])
    peer_sums = column_sums(peer_up[...])
    hid_peer[...] = hidden_of(peer_up[...], peer_sums)
    arrived(FDN, peer_down.at[pl.ds(0, hidden // 2)])
    pairs = groups // 2
    for i in range(pairs):
        pair = lax.rem(grp // 2 + 1 + i, pairs)
        columns = pl.ds(pl.multiple_of(pair * 2 * C, 2 * C), 2 * C)
        part = dot(hid_own[...], down[:, columns]) + dot(hid_peer[...], peer_down[:, columns])
        rs_send[2 * pair] = part[:, :C].astype(BF16)
        rs_send[2 * pair + 1] = part[:, C:].astype(BF16)
        if i < pairs - 1:
            for g in (2 * pair, 2 * pair + 1):
                send(rs_send.at[g], rs_recv.at[grp], RS, (row, g))
    other = grp + 1 - 2 * (grp % 2)
    send(rs_send.at[other], rs_recv.at[grp], RS, (row, other))
    rs_recv[grp] = rs_send[grp]

    for at, halo in ((HUP, halo_up), (HDN, halo_down), (HLF, halo_left), (HRT, halo_right)):
        arrived(at, halo)
    tile_rows = now.shape[1]
    row_at = lax.broadcasted_iota(jnp.int32, (tile_rows, lanes), 0)
    lane_at = lax.broadcasted_iota(jnp.int32, (tile_rows, lanes), 1)
    own = [now[0], now[1]]
    base = []
    for comp in range(2):
        above = jnp.where(row == 0, 0.0, halo_up[comp, 7:8, :])
        below = jnp.where(row == rows - 1, 0.0, halo_down[comp, 0:1, :])
        left = jnp.where(grp == 0, 0.0, halo_left[comp, :, C - 1 : C])
        right = jnp.where(grp == groups - 1, 0.0, halo_right[comp, :, 0:1])
        center = own[comp]
        up_shift = jnp.where(row_at == tile_rows - 1, below, jnp.roll(center, -1, axis=0))
        down_shift = jnp.where(row_at == 0, above, jnp.roll(center, 1, axis=0))
        from_right = jnp.where(lane_at == lanes - 1, right, jnp.roll(center, -1, axis=1))
        from_left = jnp.where(lane_at == 0, left, jnp.roll(center, 1, axis=1))
        laplace = up_shift + down_shift + from_right + from_left - 4.0 * center
        rotated = own[1] if comp == 0 else -own[0]
        base.append(center + time_step * (coriolis * rotated + viscosity * laplace))

    arrived(RS, rs_recv.at[pl.ds(0, groups - 1)])
    for r in range(2):
        values = rs_recv[r * across].astype(F32)
        for i in range(1, across):
            values = values + rs_recv[r * across + i].astype(F32)
        bo[r] = (mixed[r] + values).astype(BF16)
    tile = width // groups

    def tokens_of(g):
        return bo.at[:, pl.ds(pl.multiple_of(g * tile, tile), tile)]

    for g in g_peers:
        send(tokens_of(g), bo_recv.at[grp], BO, (row, g))
    out_copy = pltpu.make_async_copy(bo, bo_hbm, out_sem.at[0])
    out_copy.start()
    bo_recv[grp] = bo[:, pl.ds(pl.multiple_of(grp * tile, tile), tile)]
    arrived(HW, hw_recv.at[pl.ds(0, groups - 1)])
    arrived(BO, bo_recv.at[pl.ds(0, groups - 1)])
    velocity = jnp.zeros((C, 2 * tile), F32)
    for g in range(0, groups, 2):
        weights = jnp.concatenate([hw_recv[g], hw_recv[g + 1]], axis=1)
        values = jnp.concatenate(
            [bo_recv[g].reshape(2 * tile, C), bo_recv[g + 1].reshape(2 * tile, C)], axis=1
        )
        velocity = velocity + dot_nt(weights, values)

    wide = 2 * lanes
    source = lax.broadcasted_iota(jnp.int32, (2 * tile, wide), 0)
    target = lax.broadcasted_iota(jnp.int32, (2 * tile, wide), 1) // PATCH
    spread = jnp.where(source == target, 1.0, 0.0).astype(BF16)
    vel_hi, vel_lo = split_hi_lo(velocity)
    spread_out = dot(vel_hi, spread) + dot(vel_lo, spread)
    x_row = lax.broadcasted_iota(jnp.int32, (C, wide), 0) % PATCH
    x_lane = lax.broadcasted_iota(jnp.int32, (C, wide), 1) % PATCH
    kept = jnp.where(x_row == x_lane, spread_out, 0.0).reshape(C // PATCH, PATCH, wide)
    cells = jnp.sum(kept, axis=1)
    relative = []
    for comp in range(2):
        part = cells[comp * PATCH : (comp + 1) * PATCH]
        ice_vel = jnp.concatenate([part[:, :lanes], part[:, lanes:]], axis=0)
        relative.append(ice_vel - own[comp])
    speed = jnp.sqrt(relative[0] * relative[0] + relative[1] * relative[1] + speed_floor)
    drag = (time_step * drag_coef) * ice[...].astype(F32) * speed
    open_water = land[...].astype(F32)
    for comp in range(2):
        ocean[comp] = open_water * (base[comp] + drag * relative[comp])
    ocean_copy = pltpu.make_async_copy(ocean, oc_hbm, out_sem.at[1])
    ocean_copy.start()

    for at, like in drains:
        wait_on(send_sem.at[at], like)
    out_copy.wait()
    ocean_copy.wait()


def body(tokens, spec_first, spec_second, up_weight, down_weight, head_weight, ocean_vel, land_mask, ice_mask):
    planes = lax.axis_size("row") // 4
    groups = lax.axis_size("grp")
    _, width, _ = tokens.shape
    embed, hidden = up_weight.shape
    _, tile_rows, lanes = ocean_vel.shape
    size, quarter, tile = 16 * planes, 4 * planes, width // groups
    tables = jnp.asarray(dft_tables(planes))
    args = (
        tokens, spec_first, spec_second, up_weight, down_weight, head_weight, ocean_vel, land_mask, ice_mask, tables,
    )
    copies = [pltpu.VMEM(a.shape, a.dtype) for a in args]
    scratch = copies + [
        pltpu.VMEM((8, width), F32),
        pltpu.VMEM((groups, 8, width), F32),
        pltpu.VMEM((planes, 16, 2 * C), BF16),
        pltpu.VMEM((planes, 16, 2 * C), BF16),
        pltpu.VMEM((4, quarter, 2 * C), BF16),
        pltpu.VMEM((4, quarter, 2 * C), BF16),
        pltpu.VMEM((4, quarter, 2 * C), BF16),
        pltpu.VMEM((4, quarter, 2 * C), BF16),
        pltpu.VMEM((planes, 16, 2 * C), BF16),
        pltpu.VMEM((planes, 16, 2 * C), BF16),
        pltpu.VMEM((2, width, C), F32),
        pltpu.VMEM((2, width, C), BF16),
        pltpu.VMEM((groups, width, C), BF16),
        pltpu.VMEM((2, 8, width), F32),
        pltpu.VMEM((groups, 8, width), F32),
        pltpu.VMEM((embed, hidden), BF16),
        pltpu.VMEM((hidden, embed), BF16),
        pltpu.VMEM((width, hidden), BF16),
        pltpu.VMEM((width, hidden), BF16),
        pltpu.VMEM((groups, width, C), BF16),
        pltpu.VMEM((groups, width, C), BF16),
        pltpu.VMEM((2, width, C), BF16),
        pltpu.VMEM((groups, 2, tile, C), BF16),
        pltpu.VMEM((C, C), BF16),
        pltpu.VMEM((groups, C, C), BF16),
        pltpu.VMEM((2, tile_rows, lanes), F32),
        pltpu.VMEM((2, 8, lanes), F32),
        pltpu.VMEM((2, 8, lanes), F32),
        pltpu.VMEM((2, tile_rows, C), F32),
        pltpu.VMEM((2, tile_rows, C), F32),
        pltpu.VMEM((2, tile_rows, lanes), F32),
        pltpu.SemaphoreType.DMA((len(args),)),
        pltpu.SemaphoreType.DMA((18,)),
        pltpu.SemaphoreType.DMA((18,)),
        pltpu.SemaphoreType.DMA((2,)),
    ]
    return pl.pallas_call(
        functools.partial(kernel, planes, groups),
        out_shape=(
            jax.ShapeDtypeStruct(tokens.shape, BF16),
            jax.ShapeDtypeStruct(ocean_vel.shape, F32),
        ),
        in_specs=[pl.BlockSpec(memory_space=pl.ANY)] * len(args),
        out_specs=[pl.BlockSpec(memory_space=pl.ANY)] * 2,
        scratch_shapes=scratch,
        compiler_params=pltpu.CompilerParams(
            collective_id=0, has_side_effects=True, vmem_limit_bytes=40 * 1024 * 1024
        ),
    )(*args)


def solution(mesh):
    placed = (
        P("row", None, "grp"),
        P(None, "grp", None),
        P(None, "grp", None),
        P(None, "grp"),
        P("grp", None),
        P("grp", None),
        P(None, "row", "grp"),
        P("row", "grp"),
        P("row", "grp"),
    )
    return jax.shard_map(
        body,
        mesh=mesh,
        in_specs=placed,
        out_specs=(P("row", None, "grp"), P(None, "row", "grp")),
        check_vma=False,
    )
```

time: 460 us -> 84.3 us (0.18)
  the two profiles are of different devices: /device:TPU:6 before, /device:TPU:32 now
where the time goes in v1:
time: 84.3 us; the launch traced here: 83.8 us
  Pallas kernels  72.6 us (86%)
  local copies, waits for them, and re-layouts  10.5 us (12%)
    pallas_call x1, Pallas kernels, body(): pl.pallas_call(functools.partial(kernel, planes, groups), out_shape=(jax....  72.6 us
    unnamed x22, local copies, waits for them, and re-layouts  10.5 us

profile of v1, /device:TPU:32, one launch (start us, length us, event | category | flops | bytes accessed | tf_op | source)
XLA Modules:
  0.0 83.8 jit_solution(2768477903515269223)
XLA Ops:
  0.6 0.0 copy-start
  0.6 1.2 %copy-done = bf16[1024,512]{1,0:T(8,128)(2,1)S(1)} copy-done((bf16[1024,512]{1,0:T(8,128)(2,1)S(1)}, bf16[1024,512]{1,0:T(8,128)(2,1)}, u32[]{:S(2)}) %copy-start) | copy-done | bytes 1048600
  1.9 0.0 copy-start.1
  1.9 1.2 %copy-done.1 = bf16[512,1024]{1,0:T(8,128)(2,1)S(1)} copy-done((bf16[512,1024]{1,0:T(8,128)(2,1)S(1)}, bf16[512,1024]{1,0:T(8,128)(2,1)}, u32[]{:S(2)}) %copy-start.1) | copy-done | bytes 1048600
  3.1 0.0 copy-start.2
  3.1 1.1 %copy-done.2 = bf16[1536,256]{1,0:T(8,128)(2,1)S(1)} copy-done((bf16[1536,256]{1,0:T(8,128)(2,1)S(1)}, bf16[1536,256]{1,0:T(8,128)(2,1)}, u32[]{:S(2)}) %copy-start.2) | copy-done | bytes 786456
  4.2 0.0 copy-start.3
  4.2 0.9 %copy-done.3 = bf16[2,256,128]{2,1,0:T(8,128)(2,1)S(1)} copy-done((bf16[2,256,128]{2,1,0:T(8,128)(2,1)S(1)}, bf16[2,256,128]{2,1,0:T(8,128)(2,1)}, u32[]{:S(2)}) %copy-start.3) | copy-done | bytes 131096
  5.1 0.0 copy-start.4
  5.1 0.9 %copy-done.4 = f32[2,128,128]{2,1,0:T(8,128)S(1)} copy-done((f32[2,128,128]{2,1,0:T(8,128)S(1)}, f32[2,128,128]{2,1,0:T(8,128)}, u32[]{:S(2)}) %copy-start.4) | copy-done | bytes 131096
  6.0 0.0 copy-start.5
  6.0 0.9 %copy-done.5 = f32[2,128,128]{2,1,0:T(8,128)S(1)} copy-done((f32[2,128,128]{2,1,0:T(8,128)S(1)}, f32[2,128,128]{2,1,0:T(8,128)}, u32[]{:S(2)}) %copy-start.5) | copy-done | bytes 131096
  6.9 0.0 copy-start.6
  6.9 0.8 copy-done.6
  7.7 0.0 copy-start.7
  7.7 0.8 copy-done.7
  8.4 0.0 copy-start.8
  8.5 0.7 copy-done.8
  9.2 0.0 copy-start.9
  9.2 0.7 copy-done.9
  9.9 72.6 %shard_map.113 = (bf16[2,256,128]{2,1,0:T(8,128)(2,1)S(1)}, f32[2,16,256]{2,1,0:T(8,128)S(1)}) custom-call(bf16[2,256,128]{2,1,0:T(8,128)(2,1)S(1)} %copy-done.3, f32[2,128,128]{2,1,0:T(8,128)S(1)} %copy-done.4, f32[2,128,128]{2,1,0:T(8,128)S(1)} %copy-done.5, bf16[1024,512]{1,0:T(8,128)(2,1)S(1)} %copy-done, bf16[512,1024]{1,0:T(8,128)(2,1)S(1)} %copy-done.1, ...), custom_call_target="tpu_custom_call" | custom-call | tf_op jit(solution)/shard_map/pallas_call | solution.py:493
  82.5 0.7 copy.14
  83.2 0.6 copy.15
Async XLA Ops:
  0.6 1.2 %copy-start = (bf16[1024,512]{1,0:T(8,128)(2,1)S(1)}, bf16[1024,512]{1,0:T(8,128)(2,1)}, u32[]{:S(2)}) copy-start(bf16[1024,512]{1,0:T(8,128)(2,1)} %up_hbm.1) | copy-start | bytes 3145732
  1.9 1.2 %copy-start.1 = (bf16[512,1024]{1,0:T(8,128)(2,1)S(1)}, bf16[512,1024]{1,0:T(8,128)(2,1)}, u32[]{:S(2)}) copy-start(bf16[512,1024]{1,0:T(8,128)(2,1)} %down_hbm.1) | copy-start | bytes 3145732
  3.1 1.1 %copy-start.2 = (bf16[1536,256]{1,0:T(8,128)(2,1)S(1)}, bf16[1536,256]{1,0:T(8,128)(2,1)}, u32[]{:S(2)}) copy-start(bf16[1536,256]{1,0:T(8,128)(2,1)} %constant.2.clone.tab_hbm) | copy-start | bytes 2359300
  4.2 0.9 %copy-start.3 = (bf16[2,256,128]{2,1,0:T(8,128)(2,1)S(1)}, bf16[2,256,128]{2,1,0:T(8,128)(2,1)}, u32[]{:S(2)}) copy-start(bf16[2,256,128]{2,1,0:T(8,128)(2,1)} %tok_hbm.1) | copy-start | bytes 393220
  5.1 0.9 %copy-start.4 = (f32[2,128,128]{2,1,0:T(8,128)S(1)}, f32[2,128,128]{2,1,0:T(8,128)}, u32[]{:S(2)}) copy-start(f32[2,128,128]{2,1,0:T(8,128)} %first_hbm.1) | copy-start | bytes 393220
  6.0 0.9 %copy-start.5 = (f32[2,128,128]{2,1,0:T(8,128)S(1)}, f32[2,128,128]{2,1,0:T(8,128)}, u32[]{:S(2)}) copy-start(f32[2,128,128]{2,1,0:T(8,128)} %second_hbm.1) | copy-start | bytes 393220
  6.9 0.8 copy-start.6
  7.7 0.8 copy-start.7
  8.4 0.7 copy-start.8
  9.2 0.7 copy-start.9

commit v2 on v1

v2 whole, which is shorter than its diff:
```python
import functools
import math

import jax
import jax.numpy as jnp
import ml_dtypes
import numpy as np
from jax import lax
from jax.experimental import pallas as pl
from jax.experimental.pallas import tpu as pltpu
from jax.sharding import PartitionSpec as P

PATCH = 8
C = 128

epsilon = 1e-05
shrink_level = 0.01
drag_coef = 0.25
time_step = 0.5
coriolis = 0.3
viscosity = 1.0
speed_floor = 0.01

F32 = jnp.float32
BF16 = jnp.bfloat16
MESH = pl.DeviceIdType.MESH


def dft_tables(rows):
    height, width = 2 * rows, 4 * rows
    d, r, kk, part = (v.reshape(-1, 1) for v in np.meshgrid(range(rows), range(2), range(2), range(2), indexing="ij"))
    k = 2 * d + kk
    r_col, w = (v.reshape(1, -1) for v in np.meshgrid(range(2), range(width), indexing="ij"))
    angle = 2.0 * np.pi * ((k * w) % width) / width
    row_fwd = np.where(r == r_col, np.where(part == 0, np.cos(angle), -np.sin(angle)), 0.0)
    row_bwd = (np.where(k == 0, 1.0, 2.0) * row_fwd).T
    kk_row, part_row, a = (
        v.reshape(-1, 1) for v in np.meshgrid(range(2), range(2), range(height), indexing="ij")
    )
    h, kk, part = (2 * d + r).T, kk.T, part.T
    angle = 2.0 * np.pi * ((a * h) % height) / height
    cos, sin = np.cos(angle), np.sin(angle)
    real = np.where(part == 0, cos, sin)
    imag = np.where(part == 0, -sin, cos)
    col_fwd = np.where(kk_row == kk, np.where(part_row == 0, real, imag), 0.0)
    return np.stack([row_fwd, col_fwd, col_fwd.T, row_bwd]).astype(ml_dtypes.bfloat16)


def dot(a, b):
    return jnp.dot(a, b, preferred_element_type=F32)


def dot_nt(a, b):
    return lax.dot_general(a, b, (((1,), (1,)), ((), ())), preferred_element_type=F32)


def split_hi_lo(values):
    hi = values.astype(BF16)
    return hi, (values - hi.astype(F32)).astype(BF16)


def soft_shrink(values):
    return values - jnp.clip(values, -shrink_level, shrink_level)


def gelu(values):
    return 0.5 * values * (1.0 + lax.erf(values * (1.0 / math.sqrt(2.0))))


def far_first(count):
    return sorted(range(1, count), key=lambda i: -min(i, count - i))


def complex_matrix(ref):
    real, imag = ref[0], ref[1]
    top = jnp.concatenate([real, imag], axis=1)
    low = jnp.concatenate([-imag, real], axis=1)
    return jnp.concatenate([top, low], axis=0)


def stack_rows(rows, count, width):
    at = lax.broadcasted_iota(jnp.int32, (count, width), 0)
    out = jnp.zeros((count, width), F32)
    for i, values in enumerate(rows):
        out = jnp.where(at == i, values, out)
    return out


def stack_halves(rows, width):
    half = width // 2
    return stack_rows([part for values in rows for part in (values[:, :half], values[:, half:])], 8, half)


def whole_row(values, i):
    return jnp.concatenate([values[2 * i : 2 * i + 1], values[2 * i + 1 : 2 * i + 2]], axis=1)


def columns_of(rows, width):
    top = stack_rows(rows, 8, width)
    return jnp.concatenate([top, jnp.zeros((C - 8, width), F32)], axis=0).T


def kernel(
    rows,
    groups,
    tok_hbm, first_hbm, second_hbm, up_hbm, down_hbm, head_hbm, vel_hbm, land_hbm, ice_hbm, tab_hbm,
    bo_hbm, oc_hbm,
    tok, first, second, up, down, head, vel, land, ice, tab,
    st1_send, st1_recv, z1_send, z1_recv, z2_send, z2_recv,
    mixed, y_send, y_recv, st2_send, st2_recv, peer_up, peer_down, rs_send, rs_recv,
    bo, vf_send, vf_recv, hw_recv, now, halo_up, halo_down, halo_left, halo_right, ocean,
    local_sem, send_sem, recv_sem, out_sem,
):
    width = tok.shape[1]
    total_channels = C * groups
    row, grp = lax.axis_index("row"), lax.axis_index("grp")
    core, side = row % 2, grp % 2
    hidden = up.shape[1]

    r_peers = [lax.rem(row + i, rows) for i in far_first(rows)]
    g_peers = [lax.rem(grp + i, groups) for i in far_first(groups)]
    row_above, row_below = lax.rem(row + rows - 1, rows), lax.rem(row + 1, rows)
    weight_peer = (row, grp + 1 - 2 * side)
    sibling = (row + 1 - 2 * core, grp)
    greeted = [(r, grp) for r in r_peers] + [(row, g) for g in g_peers]
    barrier = pltpu.get_barrier_semaphore()
    for peer in greeted:
        pl.semaphore_signal(barrier, inc=1, device_id=peer, device_id_type=MESH)

    loads = {}
    for i, (name, src, dst) in enumerate(
        [
            ("tok", tok_hbm, tok),
            ("vel", vel_hbm, vel),
            ("land", land_hbm, land),
            ("head", head_hbm, head),
            ("tab0", tab_hbm.at[0], tab.at[0]),
            ("first", first_hbm, first),
            ("second", second_hbm, second),
            ("tab1", tab_hbm.at[1], tab.at[1]),
            ("tab2", tab_hbm.at[2], tab.at[2]),
            ("tab3", tab_hbm.at[3], tab.at[3]),
            ("up", up_hbm, up),
            ("down", down_hbm, down),
            ("ice", ice_hbm, ice),
        ]
    ):
        loads[name] = pltpu.make_async_copy(src, dst, local_sem.at[i])
        loads[name].start()

    ones = jnp.ones((16, C), BF16)
    loads["tok"].wait()
    sums = []
    squares = []
    for r in range(2):
        values = tok[r]
        wide = values.astype(F32)
        hi, lo = split_hi_lo(wide * wide)
        sums.append(dot_nt(ones, values)[0:1])
        squares.append((dot_nt(ones, hi) + dot_nt(ones, lo))[0:1])
    st1_send[...] = stack_halves(sums + squares, width)
    st1_recv[grp] = st1_send[...]
    loads["head"].wait()
    hw_recv[grp] = head[...]
    loads["vel"].wait()
    loads["land"].wait()
    open_water = land[...].astype(F32)
    now[0] = vel[0] * open_water
    now[1] = vel[1] * open_water

    pl.semaphore_wait(barrier, len(greeted))

    drains = []

    def send(src, dst, at, peer):
        pltpu.make_async_remote_copy(
            src_ref=src,
            dst_ref=dst,
            send_sem=send_sem.at[at],
            recv_sem=recv_sem.at[at],
            device_id=peer,
            device_id_type=MESH,
        ).start()

    def wait_on(sem, like):
        pltpu.make_async_copy(like, like, sem).wait()

    def arrived(at, like):
        wait_on(recv_sem.at[at], like)
        drains.append((at, like))

    ST1, WUP, WDN, HW, HUP, HDN, HLF, HRT, ST2, FUP, FDN, RS, VF = range(13)
    Z1, Z2, Y = 13, 14, (15, 16)

    for g in g_peers:
        send(st1_send, st1_recv.at[grp], ST1, (row, g))
    half_up = pl.ds(pl.multiple_of(core * (up.shape[0] // 2), up.shape[0] // 2), up.shape[0] // 2)
    half_dn = pl.ds(pl.multiple_of(core * (hidden // 2), hidden // 2), hidden // 2)
    send(up_hbm.at[half_up], peer_up.at[half_up], WUP, weight_peer)
    send(down_hbm.at[half_dn], peer_down.at[half_dn], WDN, weight_peer)

    arrived(ST1, st1_recv.at[pl.ds(0, groups - 1)])
    totals = st1_recv[0]
    for g in range(1, groups):
        totals = totals + st1_recv[g]
    totals = totals / total_channels
    mean = [whole_row(totals, r) for r in range(2)]
    scale = [lax.rsqrt(whole_row(totals, 2 + r) - mean[r] * mean[r] + epsilon) for r in range(2)]
    stats = columns_of(mean + scale, width)
    loads["tab0"].wait()
    normed = []
    for r in range(2):
        inputs = tok[r].astype(F32)
        normed.append((inputs - stats[:, r : r + 1]) * stats[:, 2 + r : 3 + r])
        mixed[r] = inputs + normed[r]

    height, size = 2 * rows, 8 * rows
    row_scale, col_scale = 1.0 / math.sqrt(width), 1.0 / math.sqrt(height)
    flat = jnp.concatenate([normed[0].astype(BF16), normed[1].astype(BF16)], axis=0)
    z1_send[...] = (dot(tab[0], flat) * row_scale).reshape(rows, 8, C).astype(BF16)
    for r in r_peers:
        send(z1_send.at[r], z1_recv.at[row], Z1, (r, grp))
    z1_recv[row] = z1_send[row]

    for g in g_peers:
        send(head, hw_recv.at[grp], HW, (row, g))
    send(now.at[:, pl.ds(8, 8)], halo_up, HUP, (row_below, grp))
    send(now.at[:, pl.ds(0, 8)], halo_down, HDN, (row_above, grp))
    lanes = now.shape[2]
    send(now.at[:, :, pl.ds(lanes - C, C)], halo_left, HLF, (row, lax.rem(grp + 1, groups)))
    send(now.at[:, :, pl.ds(0, C)], halo_right, HRT, (row, lax.rem(grp + groups - 1, groups)))
    loads["first"].wait()
    loads["second"].wait()
    weight_one = complex_matrix(first).astype(BF16)
    weight_two, weight_two_lo = split_hi_lo(complex_matrix(second))
    loads["up"].wait()
    loads["down"].wait()
    loads["ice"].wait()
    for i in range(1, 4):
        loads["tab" + str(i)].wait()
    block_at = lax.broadcasted_iota(jnp.int32, (16, total_channels), 0)
    block_of = lax.broadcasted_iota(jnp.int32, (16, total_channels), 1) // C
    pick = jnp.where(block_at == block_of, 1.0, 0.0).astype(BF16)

    def column_sums(weights):
        sums = dot(pick, weights)
        hi, lo = split_hi_lo(sums)
        pad = jnp.zeros((C - 16, weights.shape[1]), BF16)
        return jnp.concatenate([hi, pad], axis=0), jnp.concatenate([lo, pad], axis=0)

    def through(columns, sums):
        return dot(columns[0], sums[0]) + dot(columns[1], sums[0]) + dot(columns[0], sums[1])

    own_sums = column_sums(up[...])

    def blocks(values):
        return [values[i * height : (i + 1) * height] for i in range(4)]

    arrived(Z1, z1_recv.at[pl.ds(0, rows - 1)])
    columns = z1_recv[...].astype(F32).reshape(size, C).astype(BF16)
    freq = blocks((dot(tab[1], columns) * col_scale).astype(BF16))
    freq = jnp.concatenate(
        [jnp.concatenate(freq[:2], axis=1), jnp.concatenate(freq[2:], axis=1)], axis=0
    )
    hid = jax.nn.relu(dot(freq, weight_one)).astype(BF16)
    mix = soft_shrink(dot(hid, weight_two) + dot(hid, weight_two_lo)).astype(BF16)
    mix = jnp.concatenate(
        [mix[kk * height : (kk + 1) * height, p * C : (p + 1) * C] for kk in range(2) for p in range(2)], axis=0
    )
    z2_send[...] = (dot(tab[2], mix) * col_scale).reshape(rows, 8, C).astype(BF16)
    for r in r_peers:
        send(z2_send.at[r], z2_recv.at[row], Z2, (r, grp))
    z2_recv[row] = z2_send[row]

    arrived(Z2, z2_recv.at[pl.ds(0, rows - 1)])
    columns = z2_recv[...].astype(F32).reshape(size, C).astype(BF16)
    square_ones = jnp.ones((C, C), BF16)
    for r in range(2):
        values = mixed[r] + dot(tab[3, r * width : (r + 1) * width], columns) * row_scale
        mixed[r] = values
        hi = values.astype(BF16)
        local_mean = dot(hi, square_ones) * (1.0 / C)
        centered = (values - local_mean).astype(BF16)
        y_send[r] = centered
        wide = centered.astype(F32)
        sq_hi, sq_lo = split_hi_lo(wide * wide)
        row_mean = dot_nt(ones, hi)[0:1] * (1.0 / C)
        row_sum = dot_nt(ones, centered)[0:1]
        row_square = (dot_nt(ones, sq_hi) + dot_nt(ones, sq_lo))[0:1]
        st2_send[r] = stack_halves([row_mean, row_sum, row_square], width)
    for g in g_peers:
        send(st2_send.at[g % 2], st2_recv.at[grp], ST2, (row, g))
    part = width // 2
    for t in range(2):
        for g in g_peers:
            send(y_send.at[g % 2, pl.ds(t * part, part)], y_recv.at[t, grp], Y[t], (row, g))
        y_recv[t, grp] = y_send[side, t * part : (t + 1) * part]
    st2_recv[grp] = st2_send[side]

    tile = width // groups

    wait_on(recv_sem.at[WUP], peer_up.at[pl.ds(0, up.shape[0] // 2)])
    drains.append((WUP, peer_up.at[pl.ds(0, up.shape[0] // 2)]))
    send(peer_up.at[half_up], peer_up.at[half_up], FUP, sibling)
    wait_on(recv_sem.at[WDN], peer_down.at[pl.ds(0, hidden // 2)])
    drains.append((WDN, peer_down.at[pl.ds(0, hidden // 2)]))
    send(peer_down.at[half_dn], peer_down.at[half_dn], FDN, sibling)

    arrived(HW, hw_recv.at[pl.ds(0, groups - 1)])
    whole_head = hw_recv[...].reshape(total_channels, C)
    head_sums = column_sums(whole_head)
    own_head = dot(down[...], whole_head).astype(BF16)
    arrived(FUP, peer_up.at[pl.ds(0, up.shape[0] // 2)])
    peer_sums = column_sums(peer_up[...])
    arrived(FDN, peer_down.at[pl.ds(0, hidden // 2)])
    peer_head = dot(peer_down[...], whole_head).astype(BF16)
    arrived(ST2, st2_recv.at[pl.ds(0, groups - 1)])
    sent = [[whole_row(st2_recv[g], i) for i in range(3)] for g in range(groups)]
    mean = jnp.zeros((1, width), F32)
    for row_mean, row_sum, _ in sent:
        mean = mean + (row_mean + row_sum * (1.0 / C))
    mean = mean * (1.0 / groups)
    offsets = [row_mean - mean for row_mean, _, _ in sent]
    square = jnp.zeros((1, width), F32)
    for offset, (_, row_sum, row_square) in zip(offsets, sent):
        square = square + (row_square + 2.0 * offset * row_sum + float(C) * offset * offset)
    scale = lax.rsqrt(square / total_channels + epsilon)
    local_means = split_hi_lo(columns_of([row_mean for row_mean, _, _ in sent], width))
    offsets = split_hi_lo(columns_of(offsets, width))
    scale = columns_of([scale], width)[:, 0:1]

    other = weight_peer[1]
    pairs = groups // 2
    for t in range(2):
        arrived(Y[t], y_recv.at[t, pl.ds(0, groups - 1)])
        flat = jnp.concatenate([y_recv[t, g] for g in range(groups)], axis=1)
        rows_at = slice(t * part, (t + 1) * part)

        def hidden_of(weights, sums):
            shift = through([part_of[rows_at] for part_of in offsets], sums)
            return gelu((dot(flat, weights) + shift) * scale[rows_at]).astype(BF16)

        hid_own = hidden_of(up[...], own_sums)
        hid_peer = hidden_of(peer_up[...], peer_sums)

        velocity = dot(hid_own, own_head) + dot(hid_peer, peer_head)
        before = dot(flat, whole_head) + through([part_of[rows_at] for part_of in local_means], head_sums)
        tiles = range(t * (groups // 2), (t + 1) * (groups // 2))
        for i, g in enumerate(tiles):
            tokens_at = slice(i * tile, (i + 1) * tile)
            mine = jnp.where(grp // 2 == g // 2, 1.0, 0.0)
            vf_send[g] = (velocity[tokens_at] + mine * before[tokens_at]).astype(BF16)
        for g in tiles:

            @pl.when(grp != g)
            def _():
                send(vf_send.at[g], vf_recv.at[grp], VF, (row, g))

        for i in range(pairs):
            pair = lax.rem(grp // 2 + 1 + i, pairs)
            columns = pl.ds(pl.multiple_of(pair * 2 * C, 2 * C), 2 * C)
            partial = dot(hid_own, down[:, columns]) + dot(hid_peer, peer_down[:, columns])
            partial = partial.astype(BF16)
            rs_send[2 * pair, rows_at] = partial[:, :C]
            rs_send[2 * pair + 1, rows_at] = partial[:, C:]
            if i < pairs - 1:
                for g in (2 * pair, 2 * pair + 1):
                    send(rs_send.at[g, pl.ds(t * part, part)], rs_recv.at[grp, pl.ds(t * part, part)], RS, (row, g))
        send(rs_send.at[other, pl.ds(t * part, part)], rs_recv.at[grp, pl.ds(t * part, part)], RS, (row, other))
    vf_recv[grp] = vf_send[grp]
    rs_recv[grp] = rs_send[grp]

    for at, halo in ((HUP, halo_up), (HDN, halo_down), (HLF, halo_left), (HRT, halo_right)):
        arrived(at, halo)
    tile_rows = now.shape[1]
    row_at = lax.broadcasted_iota(jnp.int32, (tile_rows, lanes), 0)
    lane_at = lax.broadcasted_iota(jnp.int32, (tile_rows, lanes), 1)
    own = [now[0], now[1]]
    base = []
    for comp in range(2):
        above = jnp.where(row == 0, 0.0, halo_up[comp, 7:8, :])
        below = jnp.where(row == rows - 1, 0.0, halo_down[comp, 0:1, :])
        left = jnp.where(grp == 0, 0.0, halo_left[comp, :, C - 1 : C])
        right = jnp.where(grp == groups - 1, 0.0, halo_right[comp, :, 0:1])
        center = own[comp]
        up_shift = jnp.where(row_at == tile_rows - 1, below, jnp.roll(center, -1, axis=0))
        down_shift = jnp.where(row_at == 0, above, jnp.roll(center, 1, axis=0))
        from_right = jnp.where(lane_at == lanes - 1, right, jnp.roll(center, -1, axis=1))
        from_left = jnp.where(lane_at == 0, left, jnp.roll(center, 1, axis=1))
        laplace = up_shift + down_shift + from_right + from_left - 4.0 * center
        rotated = own[1] if comp == 0 else -own[0]
        base.append(center + time_step * (coriolis * rotated + viscosity * laplace))

    arrived(VF, vf_recv.at[pl.ds(0, groups - 1)])
    velocity = []
    for r in range(2):
        values = jnp.zeros((tile, C), F32)
        for g in range(r, groups, 2):
            values = values + vf_recv[g].astype(F32)
        velocity.append(values)
    velocity.append(jnp.zeros((C - 2 * tile, C), F32))
    velocity = jnp.concatenate(velocity, axis=0).T

    wide = 2 * lanes
    source = lax.broadcasted_iota(jnp.int32, (C, wide), 0)
    target = lax.broadcasted_iota(jnp.int32, (C, wide), 1) // PATCH
    spread = jnp.where(source == target, 1.0, 0.0).astype(BF16)
    vel_hi, vel_lo = split_hi_lo(velocity)
    spread_out = dot(vel_hi, spread) + dot(vel_lo, spread)
    x_row = lax.broadcasted_iota(jnp.int32, (C, wide), 0) % PATCH
    x_lane = lax.broadcasted_iota(jnp.int32, (C, wide), 1) % PATCH
    kept = jnp.where(x_row == x_lane, spread_out, 0.0).reshape(C // PATCH, PATCH, wide)
    cells = jnp.sum(kept, axis=1)
    relative = []
    for comp in range(2):
        part = cells[comp * PATCH : (comp + 1) * PATCH]
        ice_vel = jnp.concatenate([part[:, :lanes], part[:, lanes:]], axis=0)
        relative.append(ice_vel - own[comp])
    speed = jnp.sqrt(relative[0] * relative[0] + relative[1] * relative[1] + speed_floor)
    drag = (time_step * drag_coef) * ice[...].astype(F32) * speed
    open_water = land[...].astype(F32)
    for comp in range(2):
        ocean[comp] = open_water * (base[comp] + drag * relative[comp])
    ocean_copy = pltpu.make_async_copy(ocean, oc_hbm, out_sem.at[1])
    ocean_copy.start()

    arrived(RS, rs_recv.at[pl.ds(0, groups - 1)])
    for r in range(2):
        values = rs_recv[r].astype(F32)
        for g in range(r + 2, groups, 2):
            values = values + rs_recv[g].astype(F32)
        bo[r] = (mixed[r] + values).astype(BF16)
    out_copy = pltpu.make_async_copy(bo, bo_hbm, out_sem.at[0])
    out_copy.start()

    for at, like in drains:
        wait_on(send_sem.at[at], like)
    out_copy.wait()
    ocean_copy.wait()


def copy_kernel(bo_in, oc_in, bo_out, oc_out, bo, oc, sem):
    loads = [pltpu.make_async_copy(bo_in, bo, sem.at[0]), pltpu.make_async_copy(oc_in, oc, sem.at[1])]
    stores = [pltpu.make_async_copy(bo, bo_out, sem.at[2]), pltpu.make_async_copy(oc, oc_out, sem.at[3])]
    for load in loads:
        load.start()
    for load, store in zip(loads, stores):
        load.wait()
        store.start()
    for store in stores:
        store.wait()


def body(tokens, spec_first, spec_second, up_weight, down_weight, head_weight, ocean_vel, land_mask, ice_mask):
    rows = lax.axis_size("row")
    groups = lax.axis_size("grp")
    _, width, _ = tokens.shape
    embed, hidden = up_weight.shape
    _, tile_rows, lanes = ocean_vel.shape
    tile = width // groups
    tables = jnp.asarray(dft_tables(rows))
    args = (
        tokens, spec_first, spec_second, up_weight, down_weight, head_weight, ocean_vel, land_mask, ice_mask, tables,
    )
    copies = [pltpu.VMEM(a.shape, a.dtype) for a in args]
    scratch = copies + [
        pltpu.VMEM((8, width // 2), F32),
        pltpu.VMEM((groups, 8, width // 2), F32),
        pltpu.VMEM((rows, 8, C), BF16),
        pltpu.VMEM((rows, 8, C), BF16),
        pltpu.VMEM((rows, 8, C), BF16),
        pltpu.VMEM((rows, 8, C), BF16),
        pltpu.VMEM((2, width, C), F32),
        pltpu.VMEM((2, width, C), BF16),
        pltpu.VMEM((2, groups, width // 2, C), BF16),
        pltpu.VMEM((2, 8, width // 2), F32),
        pltpu.VMEM((groups, 8, width // 2), F32),
        pltpu.VMEM((embed, hidden), BF16),
        pltpu.VMEM((hidden, embed), BF16),
        pltpu.VMEM((groups, width, C), BF16),
        pltpu.VMEM((groups, width, C), BF16),
        pltpu.VMEM((2, width, C), BF16),
        pltpu.VMEM((groups, tile, C), BF16),
        pltpu.VMEM((groups, tile, C), BF16),
        pltpu.VMEM((groups, C, C), BF16),
        pltpu.VMEM((2, tile_rows, lanes), F32),
        pltpu.VMEM((2, 8, lanes), F32),
        pltpu.VMEM((2, 8, lanes), F32),
        pltpu.VMEM((2, tile_rows, C), F32),
        pltpu.VMEM((2, tile_rows, C), F32),
        pltpu.VMEM((2, tile_rows, lanes), F32),
        pltpu.SemaphoreType.DMA((len(args) + 3,)),
        pltpu.SemaphoreType.DMA((17,)),
        pltpu.SemaphoreType.DMA((17,)),
        pltpu.SemaphoreType.DMA((2,)),
    ]
    outs = (
        jax.ShapeDtypeStruct(tokens.shape, BF16),
        jax.ShapeDtypeStruct(ocean_vel.shape, F32),
    )
    results = pl.pallas_call(
        functools.partial(kernel, rows, groups),
        out_shape=outs,
        in_specs=[pl.BlockSpec(memory_space=pl.ANY)] * len(args),
        out_specs=[pl.BlockSpec(memory_space=pl.ANY)] * 2,
        scratch_shapes=scratch,
        compiler_params=pltpu.CompilerParams(
            collective_id=0, has_side_effects=True, vmem_limit_bytes=60 * 1024 * 1024
        ),
    )(*args)
    return pl.pallas_call(
        copy_kernel,
        out_shape=outs,
        in_specs=[pl.BlockSpec(memory_space=pl.ANY)] * 2,
        out_specs=[pl.BlockSpec(memory_space=pl.ANY)] * 2,
        scratch_shapes=[pltpu.VMEM(out.shape, out.dtype) for out in outs] + [pltpu.SemaphoreType.DMA((4,))],
    )(*results)


def solution(mesh):
    placed = (
        P("row", None, "grp"),
        P(None, "grp", None),
        P(None, "grp", None),
        P(None, "grp"),
        P("grp", None),
        P("grp", None),
        P(None, "row", "grp"),
        P("row", "grp"),
        P("row", "grp"),
    )
    return jax.shard_map(
        body,
        mesh=mesh,
        in_specs=placed,
        out_specs=(P("row", None, "grp"), P(None, "row", "grp")),
        check_vma=False,
    )
```

time: 84.3 us -> 63.5 us (0.75)
  the two profiles are of different devices: /device:TPU:32 before, /device:TPU:6 now
where the time goes in v2:
time: 63.5 us; the launch traced here: 63.4 us
  Pallas kernels  62.7 us (99%)
  between operations  0.64 us (1%)
    pallas_call x1, Pallas kernels, body(): pl.pallas_call(functools.partial(kernel, rows, groups), out_shape=outs, i...  61.1 us
    pallas_call x1, Pallas kernels, body(): pl.pallas_call(copy_kernel, out_shape=outs, in_specs=[pl.BlockSpec(memory...  1.6 us

profile of v2, /device:TPU:6, one launch (start us, length us, event | category | flops | bytes accessed | tf_op | source)
XLA Modules:
  0.0 63.4 jit_solution(14301157285527506840)
XLA Ops:
  0.6 61.1 %shard_map.113 = (bf16[2,256,128]{2,1,0:T(8,128)(2,1)}, f32[2,16,256]{2,1,0:T(8,128)}) custom-call(bf16[2,256,128]{2,1,0:T(8,128)(2,1)} %tok_hbm.1, f32[2,128,128]{2,1,0:T(8,128)} %first_hbm.1, f32[2,128,128]{2,1,0:T(8,128)} %second_hbm.1, bf16[1024,512]{1,0:T(8,128)(2,1)} %up_hbm.1, bf16[512,1024]{1,0:T(8,128)(2,1)} %down_hbm.1, bf16[128,128]{1,0:T(8,128)(2,1)} %head_hbm.1, ...), custom_call_target="tpu_custom_call" | custom-call | tf_op jit(solution)/shard_map/pallas_call | solution.py:501
  61.8 1.6 %shard_map.114 = (bf16[2,256,128]{2,1,0:T(8,128)(2,1)}, f32[2,16,256]{2,1,0:T(8,128)}) custom-call(bf16[2,256,128]{2,1,0:T(8,128)(2,1)} %get-tuple-element.4.bo_in, f32[2,16,256]{2,1,0:T(8,128)} %get-tuple-element.5.oc_in), custom_call_target="tpu_custom_call" | custom-call | tf_op jit(solution)/shard_map/pallas_call | solution.py:511

commit v3 on v2

--- a/solution.py
+++ b/solution.py
@@ -108,7 +108,7 @@
     tok, first, second, up, down, head, vel, land, ice, tab,
     st1_send, st1_recv, z1_send, z1_recv, z2_send, z2_recv,
     mixed, y_send, y_recv, st2_send, st2_recv, peer_up, peer_down, rs_send, rs_recv,
-    bo, vf_send, vf_recv, hw_recv, now, halo_up, halo_down, halo_left, halo_right, ocean,
+    bo, means, vm_send, vm_recv, vf_send, vf_recv, hw_recv, now, halo_up, halo_down, halo_left, halo_right, ocean,
     local_sem, send_sem, recv_sem, out_sem,
 ):
     width = tok.shape[1]
@@ -117,20 +117,29 @@
     core, side = row % 2, grp % 2
     hidden = up.shape[1]
 
+    tok_load = pltpu.make_async_copy(tok_hbm, tok, local_sem.at[0])
+    tok_load.start()
+    weight_peer = (row, grp + 1 - 2 * side)
+    sibling = (row + 1 - 2 * core, grp)
     r_peers = [lax.rem(row + i, rows) for i in far_first(rows)]
+    planes = rows // 4
+    z, y_lo = row // 4, (row // 2) % 2
+    far_planes = [lax.rem(z + i, planes) * 4 for i in far_first(planes)]
+    staged_peers = []
+    for to_core in range(2):
+        staged_peers += [z_at + 2 * y_at + to_core for z_at in far_planes for y_at in range(2)]
+        staged_peers.append(z * 4 + 2 * (1 - y_lo) + to_core)
+    staged_peers.append(sibling[0])
     g_peers = [lax.rem(grp + i, groups) for i in far_first(groups)]
     row_above, row_below = lax.rem(row + rows - 1, rows), lax.rem(row + 1, rows)
-    weight_peer = (row, grp + 1 - 2 * side)
-    sibling = (row + 1 - 2 * core, grp)
     greeted = [(r, grp) for r in r_peers] + [(row, g) for g in g_peers]
     barrier = pltpu.get_barrier_semaphore()
     for peer in greeted:
         pl.semaphore_signal(barrier, inc=1, device_id=peer, device_id_type=MESH)
 
-    loads = {}
+    loads = {"tok": tok_load}
     for i, (name, src, dst) in enumerate(
         [
-            ("tok", tok_hbm, tok),
             ("vel", vel_hbm, vel),
             ("land", land_hbm, land),
             ("head", head_hbm, head),
@@ -145,7 +154,7 @@
             ("ice", ice_hbm, ice),
         ]
     ):
-        loads[name] = pltpu.make_async_copy(src, dst, local_sem.at[i])
+        loads[name] = pltpu.make_async_copy(src, dst, local_sem.at[i + 1])
         loads[name].start()
 
     ones = jnp.ones((16, C), BF16)
@@ -189,8 +198,8 @@
         wait_on(recv_sem.at[at], like)
         drains.append((at, like))
 
-    ST1, WUP, WDN, HW, HUP, HDN, HLF, HRT, ST2, FUP, FDN, RS, VF = range(13)
-    Z1, Z2, Y = 13, 14, (15, 16)
+    ST1, WUP, WDN, HW, HUP, HDN, HLF, HRT, ST2, FUP, FDN, RS, VF, VM = range(14)
+    Z1, Z2, Y = 14, 15, (16, 17, 18)
 
     for g in g_peers:
         send(st1_send, st1_recv.at[grp], ST1, (row, g))
@@ -218,7 +227,7 @@
     row_scale, col_scale = 1.0 / math.sqrt(width), 1.0 / math.sqrt(height)
     flat = jnp.concatenate([normed[0].astype(BF16), normed[1].astype(BF16)], axis=0)
     z1_send[...] = (dot(tab[0], flat) * row_scale).reshape(rows, 8, C).astype(BF16)
-    for r in r_peers:
+    for r in staged_peers:
         send(z1_send.at[r], z1_recv.at[row], Z1, (r, grp))
     z1_recv[row] = z1_send[row]
 
@@ -238,18 +247,13 @@
     loads["ice"].wait()
     for i in range(1, 4):
         loads["tab" + str(i)].wait()
-    block_at = lax.broadcasted_iota(jnp.int32, (16, total_channels), 0)
+    block_at = lax.broadcasted_iota(jnp.int32, (16, total_channels), 0) % 8
     block_of = lax.broadcasted_iota(jnp.int32, (16, total_channels), 1) // C
     pick = jnp.where(block_at == block_of, 1.0, 0.0).astype(BF16)
 
     def column_sums(weights):
-        sums = dot(pick, weights)
-        hi, lo = split_hi_lo(sums)
-        pad = jnp.zeros((C - 16, weights.shape[1]), BF16)
-        return jnp.concatenate([hi, pad], axis=0), jnp.concatenate([lo, pad], axis=0)
-
-    def through(columns, sums):
-        return dot(columns[0], sums[0]) + dot(columns[1], sums[0]) + dot(columns[0], sums[1])
+        hi, lo = split_hi_lo(dot(pick, weights))
+        return jnp.concatenate([hi[:16], lo, jnp.zeros((C - 32, weights.shape[1]), BF16)], axis=0)
 
     own_sums = column_sums(up[...])
 
@@ -290,14 +294,15 @@
         st2_send[r] = stack_halves([row_mean, row_sum, row_square], width)
     for g in g_peers:
         send(st2_send.at[g % 2], st2_recv.at[grp], ST2, (row, g))
-    part = width // 2
-    for t in range(2):
+    tile = width // groups
+    cuts = (0, 2, 5, 8) if groups == 8 else (0, groups // 2, groups)
+    parts = range(len(cuts) - 1)
+    for t in parts:
+        tokens_at = pl.ds(cuts[t] * tile, (cuts[t + 1] - cuts[t]) * tile)
         for g in g_peers:
-            send(y_send.at[g % 2, pl.ds(t * part, part)], y_recv.at[t, grp], Y[t], (row, g))
-        y_recv[t, grp] = y_send[side, t * part : (t + 1) * part]
+            send(y_send.at[g % 2, tokens_at], y_recv.at[grp, tokens_at], Y[t], (row, g))
+    y_recv[grp] = y_send[side]
     st2_recv[grp] = st2_send[side]
-
-    tile = width // groups
 
     wait_on(recv_sem.at[WUP], peer_up.at[pl.ds(0, up.shape[0] // 2)])
     drains.append((WUP, peer_up.at[pl.ds(0, up.shape[0] // 2)]))
@@ -325,31 +330,28 @@
     for offset, (_, row_sum, row_square) in zip(offsets, sent):
         square = square + (row_square + 2.0 * offset * row_sum + float(C) * offset * offset)
     scale = lax.rsqrt(square / total_channels + epsilon)
-    local_means = split_hi_lo(columns_of([row_mean for row_mean, _, _ in sent], width))
-    offsets = split_hi_lo(columns_of(offsets, width))
+    local_means = in_parts([row_mean for row_mean, _, _ in sent], width)
+    offsets = in_parts(offsets, width)
     scale = columns_of([scale], width)[:, 0:1]
 
     other = weight_peer[1]
     pairs = groups // 2
-    for t in range(2):
-        arrived(Y[t], y_recv.at[t, pl.ds(0, groups - 1)])
-        flat = jnp.concatenate([y_recv[t, g] for g in range(groups)], axis=1)
-        rows_at = slice(t * part, (t + 1) * part)
+    for t in parts:
+        rows_at = slice(cuts[t] * tile, cuts[t + 1] * tile)
+        part = pl.ds(rows_at.start, rows_at.stop - rows_at.start)
+        arrived(Y[t], y_recv.at[pl.ds(0, groups - 1), part])
+        flat = jnp.concatenate([y_recv[g, rows_at] for g in range(groups)], axis=1)
 
         def hidden_of(weights, sums):
-            shift = through([part_of[rows_at] for part_of in offsets], sums)
+            shift = dot(offsets[rows_at], sums)
             return gelu((dot(flat, weights) + shift) * scale[rows_at]).astype(BF16)
 
         hid_own = hidden_of(up[...], own_sums)
         hid_peer = hidden_of(peer_up[...], peer_sums)
 
         velocity = dot(hid_own, own_head) + dot(hid_peer, peer_head)
-        before = dot(flat, whole_head) + through([part_of[rows_at] for part_of in local_means], head_sums)
-        tiles = range(t * (groups // 2), (t + 1) * (groups // 2))
-        for i, g in enumerate(tiles):
-            tokens_at = slice(i * tile, (i + 1) * tile)
-            mine = jnp.where(grp // 2 == g // 2, 1.0, 0.0)
-            vf_send[g] = (velocity[tokens_at] + mine * before[tokens_at]).astype(BF16)
+        tiles = range(cuts[t], cuts[t + 1])
+        vf_send[tiles.start : tiles.stop] = velocity.astype(BF16).reshape(len(tiles), tile, C)
         for g in tiles:
 
             @pl.when(grp != g)
@@ -365,9 +367,17 @@
             rs_send[2 * pair + 1, rows_at] = partial[:, C:]
             if i < pairs - 1:
                 for g in (2 * pair, 2 * pair + 1):
-                    send(rs_send.at[g, pl.ds(t * part, part)], rs_recv.at[grp, pl.ds(t * part, part)], RS, (row, g))
-        send(rs_send.at[other, pl.ds(t * part, part)], rs_recv.at[grp, pl.ds(t * part, part)], RS, (row, other))
+                    send(rs_send.at[g, part], rs_recv.at[grp, part], RS, (row, g))
+        send(rs_send.at[other, part], rs_recv.at[grp, part], RS, (row, other))
     vf_recv[grp] = vf_send[grp]
+
+    mine_at = pl.ds(pl.multiple_of((grp // 2) * 2 * tile, 2 * tile), 2 * tile)
+    flat = jnp.concatenate([y_recv[g, mine_at] for g in range(groups)], axis=1)
+    means[...] = local_means
+    velocity = dot(flat, whole_head) + dot(means[mine_at], head_sums)
+    vm_send[...] = velocity.astype(BF16).reshape(2, tile, C)
+    send(vm_send.at[1 - side], vm_recv.at[side], VM, (row, other))
+    vm_recv[side] = vm_send[side]
     rs_recv[grp] = rs_send[grp]
 
     for at, halo in ((HUP, halo_up), (HDN, halo_down), (HLF, halo_left), (HRT, halo_right)):
@@ -392,9 +402,10 @@
         base.append(center + time_step * (coriolis * rotated + viscosity * laplace))
 
     arrived(VF, vf_recv.at[pl.ds(0, groups - 1)])
+    arrived(VM, vm_recv.at[0])
     velocity = []
     for r in range(2):
-        values = jnp.zeros((tile, C), F32)
+        values = vm_recv[r].astype(F32)
         for g in range(r, groups, 2):
             values = values + vf_recv[g].astype(F32)
         velocity.append(values)
@@ -439,6 +450,14 @@
     ocean_copy.wait()
 
 
+def in_parts(rows, width):
+    top = stack_rows(rows, 8, width)
+    values = jnp.concatenate([top, top, top, jnp.zeros((C - 24, width), F32)], axis=0).T
+    hi, lo = split_hi_lo(values)
+    lane = lax.broadcasted_iota(jnp.int32, values.shape, 1)
+    return jnp.where((lane >= 8) & (lane < 16), lo.astype(F32), hi.astype(F32)).astype(BF16)
+
+
 def copy_kernel(bo_in, oc_in, bo_out, oc_out, bo, oc, sem):
     loads = [pltpu.make_async_copy(bo_in, bo, sem.at[0]), pltpu.make_async_copy(oc_in, oc, sem.at[1])]
     stores = [pltpu.make_async_copy(bo, bo_out, sem.at[2]), pltpu.make_async_copy(oc, oc_out, sem.at[3])]
@@ -472,7 +491,7 @@
         pltpu.VMEM((rows, 8, C), BF16),
         pltpu.VMEM((2, width, C), F32),
         pltpu.VMEM((2, width, C), BF16),
-        pltpu.VMEM((2, groups, width // 2, C), BF16),
+        pltpu.VMEM((groups, width, C), BF16),
         pltpu.VMEM((2, 8, width // 2), F32),
         pltpu.VMEM((groups, 8, width // 2), F32),
         pltpu.VMEM((embed, hidden), BF16),
@@ -480,6 +499,9 @@
         pltpu.VMEM((groups, width, C), BF16),
         pltpu.VMEM((groups, width, C), BF16),
         pltpu.VMEM((2, width, C), BF16),
+        pltpu.VMEM((width, C), BF16),
+        pltpu.VMEM((2, tile, C), BF16),
+        pltpu.VMEM((2, tile, C), BF16),
         pltpu.VMEM((groups, tile, C), BF16),
         pltpu.VMEM((groups, tile, C), BF16),
         pltpu.VMEM((groups, C, C), BF16),
@@ -490,8 +512,8 @@
         pltpu.VMEM((2, tile_rows, C), F32),
         pltpu.VMEM((2, tile_rows, lanes), F32),
         pltpu.SemaphoreType.DMA((len(args) + 3,)),
-        pltpu.SemaphoreType.DMA((17,)),
-        pltpu.SemaphoreType.DMA((17,)),
+        pltpu.SemaphoreType.DMA((19,)),
+        pltpu.SemaphoreType.DMA((19,)),
         pltpu.SemaphoreType.DMA((2,)),
     ]
     outs = (

time: 63.5 us -> 62.9 us (level)
  Pallas kernels: 62.7 us -> 61.7 us
    pallas_call x1, Pallas kernels: 61.1 us -> 60.1 us  [body(): pl.pallas_call(functools.partial(kernel, rows, groups), out_shape=outs, i...]
where the time goes in v3:
time: 62.9 us; the launch traced here: 62.4 us
  Pallas kernels  61.7 us (98%)
  between operations  0.64 us (1%)
    pallas_call x1, Pallas kernels, body(): pl.pallas_call(functools.partial(kernel, rows, groups), out_shape=outs, i...  60.1 us
    pallas_call x1, Pallas kernels, body(): pl.pallas_call(copy_kernel, out_shape=outs, in_specs=[pl.BlockSpec(memory...  1.6 us

profile of v3, /device:TPU:6, one launch (start us, length us, event | category | flops | bytes accessed | tf_op | source)
XLA Modules:
  0.0 62.4 jit_solution(4980975125506174370)
XLA Ops:
  0.6 60.1 %shard_map.113 = (bf16[2,256,128]{2,1,0:T(8,128)(2,1)}, f32[2,16,256]{2,1,0:T(8,128)}) custom-call(bf16[2,256,128]{2,1,0:T(8,128)(2,1)} %tok_hbm.1, f32[2,128,128]{2,1,0:T(8,128)} %first_hbm.1, f32[2,128,128]{2,1,0:T(8,128)} %second_hbm.1, bf16[1024,512]{1,0:T(8,128)(2,1)} %up_hbm.1, bf16[512,1024]{1,0:T(8,128)(2,1)} %down_hbm.1, bf16[128,128]{1,0:T(8,128)(2,1)} %head_hbm.1, ...), custom_call_target="tpu_custom_call" | custom-call | tf_op jit(solution)/shard_map/pallas_call | solution.py:523
  60.8 1.6 %shard_map.114 = (bf16[2,256,128]{2,1,0:T(8,128)(2,1)}, f32[2,16,256]{2,1,0:T(8,128)}) custom-call(bf16[2,256,128]{2,1,0:T(8,128)(2,1)} %get-tuple-element.4.bo_in, f32[2,16,256]{2,1,0:T(8,128)} %get-tuple-element.5.oc_in), custom_call_target="tpu_custom_call" | custom-call | tf_op jit(solution)/shard_map/pallas_call | solution.py:533

commit v4 on v3

--- a/solution.py
+++ b/solution.py
@@ -199,7 +199,7 @@
         drains.append((at, like))
 
     ST1, WUP, WDN, HW, HUP, HDN, HLF, HRT, ST2, FUP, FDN, RS, VF, VM = range(14)
-    Z1, Z2, Y = 14, 15, (16, 17, 18)
+    Z1, Z2, Y = 14, 15, (16, 17, 18, 19)
 
     for g in g_peers:
         send(st1_send, st1_recv.at[grp], ST1, (row, g))
@@ -287,15 +287,15 @@
         centered = (values - local_mean).astype(BF16)
         y_send[r] = centered
         wide = centered.astype(F32)
-        sq_hi, sq_lo = split_hi_lo(wide * wide)
         row_mean = dot_nt(ones, hi)[0:1] * (1.0 / C)
         row_sum = dot_nt(ones, centered)[0:1]
+        sq_hi, sq_lo = split_hi_lo(wide * wide)
         row_square = (dot_nt(ones, sq_hi) + dot_nt(ones, sq_lo))[0:1]
         st2_send[r] = stack_halves([row_mean, row_sum, row_square], width)
     for g in g_peers:
         send(st2_send.at[g % 2], st2_recv.at[grp], ST2, (row, g))
     tile = width // groups
-    cuts = (0, 2, 5, 8) if groups == 8 else (0, groups // 2, groups)
+    cuts = (0, 1, 3, 5, 8) if groups == 8 else (0, groups // 2, groups)
     parts = range(len(cuts) - 1)
     for t in parts:
         tokens_at = pl.ds(cuts[t] * tile, (cuts[t + 1] - cuts[t]) * tile)
@@ -335,7 +335,6 @@
     scale = columns_of([scale], width)[:, 0:1]
 
     other = weight_peer[1]
-    pairs = groups // 2
     for t in parts:
         rows_at = slice(cuts[t] * tile, cuts[t + 1] * tile)
         part = pl.ds(rows_at.start, rows_at.stop - rows_at.start)
@@ -349,7 +348,10 @@
         hid_own = hidden_of(up[...], own_sums)
         hid_peer = hidden_of(peer_up[...], peer_sums)
 
+        partial = (dot(hid_own, down[...]) + dot(hid_peer, peer_down[...])).astype(BF16)
         velocity = dot(hid_own, own_head) + dot(hid_peer, peer_head)
+        for g in range(groups):
+            rs_send[g, rows_at] = partial[:, g * C : (g + 1) * C]
         tiles = range(cuts[t], cuts[t + 1])
         vf_send[tiles.start : tiles.stop] = velocity.astype(BF16).reshape(len(tiles), tile, C)
         for g in tiles:
@@ -358,16 +360,10 @@
             def _():
                 send(vf_send.at[g], vf_recv.at[grp], VF, (row, g))
 
-        for i in range(pairs):
-            pair = lax.rem(grp // 2 + 1 + i, pairs)
-            columns = pl.ds(pl.multiple_of(pair * 2 * C, 2 * C), 2 * C)
-            partial = dot(hid_own, down[:, columns]) + dot(hid_peer, peer_down[:, columns])
-            partial = partial.astype(BF16)
-            rs_send[2 * pair, rows_at] = partial[:, :C]
-            rs_send[2 * pair + 1, rows_at] = partial[:, C:]
-            if i < pairs - 1:
-                for g in (2 * pair, 2 * pair + 1):
-                    send(rs_send.at[g, part], rs_recv.at[grp, part], RS, (row, g))
+        for i in range(1, groups // 2):
+            pair = lax.rem(grp // 2 + i, groups // 2)
+            for g in (2 * pair, 2 * pair + 1):
+                send(rs_send.at[g, part], rs_recv.at[grp, part], RS, (row, g))
         send(rs_send.at[other, part], rs_recv.at[grp, part], RS, (row, other))
     vf_recv[grp] = vf_send[grp]
 
@@ -432,7 +428,8 @@
     open_water = land[...].astype(F32)
     for comp in range(2):
         ocean[comp] = open_water * (base[comp] + drag * relative[comp])
-    ocean_copy = pltpu.make_async_copy(ocean, oc_hbm, out_sem.at[1])
+    out_copies = []
+    ocean_copy = pltpu.make_async_copy(ocean, oc_hbm, out_sem.at[2])
     ocean_copy.start()
 
     arrived(RS, rs_recv.at[pl.ds(0, groups - 1)])
@@ -441,13 +438,13 @@
         for g in range(r + 2, groups, 2):
             values = values + rs_recv[g].astype(F32)
         bo[r] = (mixed[r] + values).astype(BF16)
-    out_copy = pltpu.make_async_copy(bo, bo_hbm, out_sem.at[0])
-    out_copy.start()
+        out_copies.append(pltpu.make_async_copy(bo.at[r], bo_hbm.at[r], out_sem.at[r]))
+        out_copies[r].start()
 
     for at, like in drains:
         wait_on(send_sem.at[at], like)
-    out_copy.wait()
-    ocean_copy.wait()
+    for copy in out_copies + [ocean_copy]:
+        copy.wait()
 
 
 def in_parts(rows, width):
@@ -458,9 +455,15 @@
     return jnp.where((lane >= 8) & (lane < 16), lo.astype(F32), hi.astype(F32)).astype(BF16)
 
 
+def quarters(ref):
+    half = ref.shape[1] // 2
+    return [ref.at[i, pl.ds(j * half, half)] for i in range(2) for j in range(2)]
+
+
 def copy_kernel(bo_in, oc_in, bo_out, oc_out, bo, oc, sem):
-    loads = [pltpu.make_async_copy(bo_in, bo, sem.at[0]), pltpu.make_async_copy(oc_in, oc, sem.at[1])]
-    stores = [pltpu.make_async_copy(bo, bo_out, sem.at[2]), pltpu.make_async_copy(oc, oc_out, sem.at[3])]
+    steps = list(zip(quarters(bo_in), quarters(bo), quarters(bo_out))) + [(oc_in, oc, oc_out)]
+    loads = [pltpu.make_async_copy(src, mid, sem.at[0, i]) for i, (src, mid, _) in enumerate(steps)]
+    stores = [pltpu.make_async_copy(mid, dst, sem.at[1, i]) for i, (_, mid, dst) in enumerate(steps)]
     for load in loads:
         load.start()
     for load, store in zip(loads, stores):
@@ -512,9 +515,9 @@
         pltpu.VMEM((2, tile_rows, C), F32),
         pltpu.VMEM((2, tile_rows, lanes), F32),
         pltpu.SemaphoreType.DMA((len(args) + 3,)),
-        pltpu.SemaphoreType.DMA((19,)),
-        pltpu.SemaphoreType.DMA((19,)),
-        pltpu.SemaphoreType.DMA((2,)),
+        pltpu.SemaphoreType.DMA((20,)),
+        pltpu.SemaphoreType.DMA((20,)),
+        pltpu.SemaphoreType.DMA((3,)),
     ]
     outs = (
         jax.ShapeDtypeStruct(tokens.shape, BF16),
@@ -535,7 +538,7 @@
         out_shape=outs,
         in_specs=[pl.BlockSpec(memory_space=pl.ANY)] * 2,
         out_specs=[pl.BlockSpec(memory_space=pl.ANY)] * 2,
-        scratch_shapes=[pltpu.VMEM(out.shape, out.dtype) for out in outs] + [pltpu.SemaphoreType.DMA((4,))],
+        scratch_shapes=[pltpu.VMEM(out.shape, out.dtype) for out in outs] + [pltpu.SemaphoreType.DMA((2, 5))],
     )(*results)
 
 

time: 62.9 us -> 62.5 us (level)
  no operation moved by 1% of the time
where the time goes in v4:
time: 62.5 us; the launch traced here: 62.3 us
  Pallas kernels  61.7 us (99%)
  between operations  0.64 us (1%)
    pallas_call x1, Pallas kernels, body(): pl.pallas_call(functools.partial(kernel, rows, groups), out_shape=outs, i...  60.1 us
    pallas_call x1, Pallas kernels, body(): pl.pallas_call(copy_kernel, out_shape=outs, in_specs=[pl.BlockSpec(memory...  1.53 us

profile of v4, /device:TPU:6, one launch (start us, length us, event | category | flops | bytes accessed | tf_op | source)
XLA Modules:
  0.0 62.3 jit_solution(16300961292531803441)
XLA Ops:
  0.6 60.1 %shard_map.113 = (bf16[2,256,128]{2,1,0:T(8,128)(2,1)}, f32[2,16,256]{2,1,0:T(8,128)}) custom-call(bf16[2,256,128]{2,1,0:T(8,128)(2,1)} %tok_hbm.1, f32[2,128,128]{2,1,0:T(8,128)} %first_hbm.1, f32[2,128,128]{2,1,0:T(8,128)} %second_hbm.1, bf16[1024,512]{1,0:T(8,128)(2,1)} %up_hbm.1, bf16[512,1024]{1,0:T(8,128)(2,1)} %down_hbm.1, bf16[128,128]{1,0:T(8,128)(2,1)} %head_hbm.1, ...), custom_call_target="tpu_custom_call" | custom-call | tf_op jit(solution)/shard_map/pallas_call | solution.py:526
  60.8 1.5 %shard_map.114 = (bf16[2,256,128]{2,1,0:T(8,128)(2,1)}, f32[2,16,256]{2,1,0:T(8,128)}) custom-call(bf16[2,256,128]{2,1,0:T(8,128)(2,1)} %get-tuple-element.4.bo_in, f32[2,16,256]{2,1,0:T(8,128)} %get-tuple-element.5.oc_in), custom_call_target="tpu_custom_call" | custom-call | tf_op jit(solution)/shard_map/pallas_call | solution.py:536

commit v5 on v4

--- a/solution.py
+++ b/solution.py
@@ -33,6 +33,7 @@
     r_col, w = (v.reshape(1, -1) for v in np.meshgrid(range(2), range(width), indexing="ij"))
     angle = 2.0 * np.pi * ((k * w) % width) / width
     row_fwd = np.where(r == r_col, np.where(part == 0, np.cos(angle), -np.sin(angle)), 0.0)
+    row_fwd = row_fwd / math.sqrt(width)
     row_bwd = (np.where(k == 0, 1.0, 2.0) * row_fwd).T
     kk_row, part_row, a = (
         v.reshape(-1, 1) for v in np.meshgrid(range(2), range(2), range(height), indexing="ij")
@@ -224,9 +225,9 @@
         mixed[r] = inputs + normed[r]
 
     height, size = 2 * rows, 8 * rows
-    row_scale, col_scale = 1.0 / math.sqrt(width), 1.0 / math.sqrt(height)
+    col_scale = 1.0 / math.sqrt(height)
     flat = jnp.concatenate([normed[0].astype(BF16), normed[1].astype(BF16)], axis=0)
-    z1_send[...] = (dot(tab[0], flat) * row_scale).reshape(rows, 8, C).astype(BF16)
+    z1_send[...] = dot(tab[0], flat).reshape(rows, 8, C).astype(BF16)
     for r in staged_peers:
         send(z1_send.at[r], z1_recv.at[row], Z1, (r, grp))
     z1_recv[row] = z1_send[row]
@@ -240,7 +241,7 @@
     send(now.at[:, :, pl.ds(0, C)], halo_right, HRT, (row, lax.rem(grp + groups - 1, groups)))
     loads["first"].wait()
     loads["second"].wait()
-    weight_one = complex_matrix(first).astype(BF16)
+    weight_one = (complex_matrix(first) * col_scale).astype(BF16)
     weight_two, weight_two_lo = split_hi_lo(complex_matrix(second))
     loads["up"].wait()
     loads["down"].wait()
@@ -262,7 +263,7 @@
 
     arrived(Z1, z1_recv.at[pl.ds(0, rows - 1)])
     columns = z1_recv[...].astype(F32).reshape(size, C).astype(BF16)
-    freq = blocks((dot(tab[1], columns) * col_scale).astype(BF16))
+    freq = blocks(dot(tab[1], columns).astype(BF16))
     freq = jnp.concatenate(
         [jnp.concatenate(freq[:2], axis=1), jnp.concatenate(freq[2:], axis=1)], axis=0
     )
@@ -280,7 +281,7 @@
     columns = z2_recv[...].astype(F32).reshape(size, C).astype(BF16)
     square_ones = jnp.ones((C, C), BF16)
     for r in range(2):
-        values = mixed[r] + dot(tab[3, r * width : (r + 1) * width], columns) * row_scale
+        values = mixed[r] + dot(tab[3, r * width : (r + 1) * width], columns)
         mixed[r] = values
         hi = values.astype(BF16)
         local_mean = dot(hi, square_ones) * (1.0 / C)

time: 62.5 us -> 62.7 us (level)
  no operation moved by 1% of the time
where the time goes in v5:
time: 62.7 us; the launch traced here: 62.2 us
  Pallas kernels  61.5 us (98%)
  between operations  0.64 us (1%)
    pallas_call x1, Pallas kernels, body(): pl.pallas_call(functools.partial(kernel, rows, groups), out_shape=outs, i...  60 us
    pallas_call x1, Pallas kernels, body(): pl.pallas_call(copy_kernel, out_shape=outs, in_specs=[pl.BlockSpec(memory...  1.53 us

profile of v5, /device:TPU:6, one launch (start us, length us, event | category | flops | bytes accessed | tf_op | source)
XLA Modules:
  0.0 62.2 jit_solution(12427981438030247998)
XLA Ops:
  0.6 60.0 %shard_map.113 = (bf16[2,256,128]{2,1,0:T(8,128)(2,1)}, f32[2,16,256]{2,1,0:T(8,128)}) custom-call(bf16[2,256,128]{2,1,0:T(8,128)(2,1)} %tok_hbm.1, f32[2,128,128]{2,1,0:T(8,128)} %first_hbm.1, f32[2,128,128]{2,1,0:T(8,128)} %second_hbm.1, bf16[1024,512]{1,0:T(8,128)(2,1)} %up_hbm.1, bf16[512,1024]{1,0:T(8,128)(2,1)} %down_hbm.1, bf16[128,128]{1,0:T(8,128)(2,1)} %head_hbm.1, ...), custom_call_target="tpu_custom_call" | custom-call | tf_op jit(solution)/shard_map/pallas_call | solution.py:527
  60.7 1.5 %shard_map.114 = (bf16[2,256,128]{2,1,0:T(8,128)(2,1)}, f32[2,16,256]{2,1,0:T(8,128)}) custom-call(bf16[2,256,128]{2,1,0:T(8,128)(2,1)} %get-tuple-element.4.bo_in, f32[2,16,256]{2,1,0:T(8,128)} %get-tuple-element.5.oc_in), custom_call_target="tpu_custom_call" | custom-call | tf_op jit(solution)/shard_map/pallas_call | solution.py:537
